TPU v7x, 32 devices: a whole 2x2x4 slice. The times are simulated.
32 devices in a mesh: tx: 8 (over y, x, core), ty: 4 (over z).
Axes of the slice: x: 2, y: 2, z: 4, core: 2. Of those that a mesh axis runs over, the one named last changes fastest.
Arguments:
- potential: float32 [8192, 768], P(('tx', 'ty')), may hold values from -3 to 3
- gating: float32 [8192, 768], P(('tx', 'ty')), may hold values from -3 to 3
- ecs_start: float32 [256, 128, 32], P('tx', 'ty'), may hold values from -6 to 6
- templates: bfloat16 [10, 768, 768], replicated, may hold values from -0.21875 to 0.21875
- template_id: int32 [8192], P(('tx', 'ty')), may hold values from 0 to 9
- patch_src: int32 [32768], P(('tx', 'ty')), may hold values from 0 to 3071
- patch_dev: int32 [32768, 1], P(('tx', 'ty')), may hold values from 0 to 31; in each aligned block of 1024 rows (0 to 1023, 1024 to 2047, ...) at most 64 rows name the same one
- patch_dst: int32 [32768], P(('tx', 'ty')), may hold values from 0 to 3071
- patch_conduct: float32 [32768], P(('tx', 'ty')), may hold values from 0.5 to 2
- memb_point: int32 [98304], P(('tx', 'ty')), may hold values from 0 to 32767
Outputs:
- final_potential: float32 [8192, 768], P(('tx', 'ty'))
- final_ecs: float32 [256, 128, 32], P('tx', 'ty')
Inputs may be any that keep to these rules, and one draw needn't show every extreme that they name: `patch_dev`: among the 1024 gap junctions listed on one device, at most 64 have their target on any one device, and some device receives exactly 64 from some device.
All inputs are finite; a program needn't handle non-finite values.
Results may differ from a plain program's by a relative error of at most 0.0003.
Values sent between devices are 32-bit elements; how exact they have to be, the bound alone decides.
A program may use at most 128 MiB of HBM per device.

v0:
```python
import jax
import jax.numpy as jnp
from jax import lax
from jax.experimental import pallas as pl
from jax.experimental.pallas import tpu as pltpu
from jax.sharding import PartitionSpec as P

BLOCK = 64
SWEEPS = 4
STEPS = 2
LANES = 128
VMEM_BYTES = 40 * 1024 * 1024


def extended(x, sides, width):
    for axis, dim in sides:
        devices, length = (lax.axis_size(axis), x.shape[dim])
        up = [(i, (i + 1) % devices) for i in range(devices - 1)]
        down = [(j, i) for i, j in up]
        last = lax.slice_in_dim(x, length - width, length, axis=dim)
        leading = lax.slice_in_dim(x, 0, width, axis=dim)
        before = lax.ppermute(last, axis, up)
        after = lax.ppermute(leading, axis, down)
        x = jnp.concatenate([before, x, after], axis=dim)
    return x


def stencil_sum(framed):
    total = framed[2:, 1:-1, 1:-1] + framed[:-2, 1:-1, 1:-1]
    total = total + framed[1:-1, 2:, 1:-1] + framed[1:-1, :-2, 1:-1]
    return total + framed[1:-1, 1:-1, 2:] + framed[1:-1, 1:-1, :-2]


def two_parts(x):
    high = x.astype(jnp.bfloat16)
    low = (x - high.astype(jnp.float32)).astype(jnp.bfloat16)
    return high, low


def dot32(a, b):
    return jnp.dot(a, b, preferred_element_type=jnp.float32)


def onehot_of(hit):
    return jnp.where(hit, 1.0, 0.0).astype(jnp.bfloat16)


def gather_kernel(volt_ref, cols_ref, out_ref, parts_ref):
    cells, nodes = volt_ref.shape
    rows = out_ref.shape[0]

    @pl.when(pl.program_id(0) == 0)
    def _():
        high, low = two_parts(volt_ref[...])
        parts_ref[0:cells, :] = high
        parts_ref[cells : 2 * cells, :] = low

    lane = lax.broadcasted_iota(jnp.int32, (rows, LANES), 1)
    cell_lane = lax.broadcasted_iota(jnp.int32, (rows, cells), 1)

    def pick(cell, spot):
        hit = onehot_of(cell_lane == cell)
        wide = dot32(jnp.concatenate([hit, hit], axis=1), parts_ref[...])
        pair = lax.shift_right_arithmetic(spot, 1)
        picked = jnp.zeros((rows, LANES), jnp.float32)
        for g in range(nodes // LANES):
            picked = jnp.where(pair == g, wide[:, g * LANES : (g + 1) * LANES], picked)
        return picked

    cols = cols_ref[...]
    spot_a, spot_b = cols[:, 1:2], cols[:, 3:4]
    a = pick(cols[:, 0:1], spot_a)
    b = pick(cols[:, 2:3], spot_b)
    a = jnp.where((spot_a & 1) == 1, pltpu.roll(a, BLOCK, 1), a)
    b = jnp.where((spot_b & 1) == 0, pltpu.roll(b, BLOCK, 1), b)
    out_ref[...] = jnp.where(lane < BLOCK, a, b)


def steklov_kernel(ident_ref, volt_ref, recov_ref, template_ref, out_ref):
    index = pl.program_id(0)
    volt = volt_ref[...]

    @pl.when(index == 0)
    def _():
        out_ref[...] = -(volt - volt * volt * volt / 3.0 - recov_ref[...])

    masked = jnp.where(ident_ref[...] == index, volt, 0.0).astype(jnp.bfloat16)
    out_ref[...] += dot32(masked, template_ref[0])


def scatter_kernel(
    got_ref, sent_ref, cols_ref, conduct_ref, cells_ref, base_ref, memb_ref, memb_t_ref, current_ref, deposit_ref, gap_ref
):
    cells, nodes = base_ref.shape
    rows = got_ref.shape[0]

    @pl.when(pl.program_id(0) == 0)
    def _():
        gap_ref[...] = jnp.zeros_like(gap_ref)

    lane = lax.broadcasted_iota(jnp.int32, (rows, LANES), 1)
    half = jnp.where(lane < BLOCK, 0, 1)
    cols = cols_ref[...]
    conduct = conduct_ref[...]
    scale = jnp.where(lane < BLOCK, conduct[:, 0:1], conduct[:, 1:2])
    flux = scale * (got_ref[...] - pltpu.roll(sent_ref[...], BLOCK, 1))
    turned = pltpu.roll(flux, BLOCK, 1)
    own_row = lax.broadcasted_iota(jnp.int32, (cells, rows), 0)

    def spread(cell_row, spot, home):
        hit = onehot_of(own_row == cell_row)
        side = spot & 1
        placed = jnp.where(half == side, jnp.where(side == home, flux, turned), 0.0)
        pair = lax.shift_right_arithmetic(spot, 1)
        total = []
        for g in range(nodes // LANES):
            high, low = two_parts(jnp.where(pair == g, placed, 0.0))
            total.append(jnp.concatenate([high, low], axis=0))
        return dot32(jnp.concatenate([hit, hit], axis=1), jnp.concatenate(total, axis=1))

    gap_ref[...] += spread(cells_ref[1:2, :], cols[:, 3:4], 0)
    gap_ref[...] += spread(cells_ref[0:1, :], cols[:, 1:2], 1)

    @pl.when(pl.program_id(0) == pl.num_programs(0) - 1)
    def _():
        current = base_ref[...] - gap_ref[...]
        current_ref[...] = current
        grid_rows = deposit_ref.shape[0]
        grid_row = lax.broadcasted_iota(jnp.int32, (grid_rows, cells), 0)
        cell_lane = lax.broadcasted_iota(jnp.int32, (cells, LANES), 1)
        total = jnp.zeros(deposit_ref.shape, jnp.float32)
        for k in range(nodes // BLOCK):
            g = k // 2
            part = current[:, g * LANES : (g + 1) * LANES]
            kept = (cell_lane < BLOCK) if k % 2 == 0 else (cell_lane >= BLOCK)
            mean = jnp.sum(jnp.where(kept, part, 0.0), axis=1, keepdims=True) * (1.0 / BLOCK)
            column = memb_ref[:, k : k + 1] & (LANES - 1)
            high, low = two_parts(jnp.where(cell_lane == column, mean, 0.0))
            hit = onehot_of(grid_row == lax.shift_right_arithmetic(memb_t_ref[k : k + 1, :], 7))
            total = total + dot32(hit, high) + dot32(hit, low)
        deposit_ref[...] = total


def update_kernel(volt_ref, recov_ref, current_ref, phi_ref, memb_ref, volt_out, recov_out):
    cells, nodes = volt_ref.shape
    grid_rows = phi_ref.shape[0]
    high, low = two_parts(phi_ref[...])
    both = jnp.concatenate([high, low], axis=0)
    lane = lax.broadcasted_iota(jnp.int32, (cells, LANES), 1)
    grid_lane = lax.broadcasted_iota(jnp.int32, (cells, grid_rows), 1)

    def value(k):
        memb = memb_ref[:, k : k + 1]
        hit = onehot_of(grid_lane == lax.shift_right_arithmetic(memb, 7))
        row = dot32(jnp.concatenate([hit, hit], axis=1), both)
        return jnp.sum(jnp.where(lane == (memb & (LANES - 1)), row, 0.0), axis=1, keepdims=True)

    for g in range(nodes // LANES):
        phi_nodes = jnp.where(lane < BLOCK, value(2 * g), value(2 * g + 1))
        span = slice(g * LANES, (g + 1) * LANES)
        volt, recov = volt_ref[:, span], recov_ref[:, span]
        recov_out[:, span] = recov + 0.05 * 0.08 * (volt + 0.7 - 0.8 * recov)
        volt_out[:, span] = volt - 0.05 * (current_ref[:, span] + phi_nodes)


def params():
    return pltpu.CompilerParams(vmem_limit_bytes=VMEM_BYTES)


def whole_block(shape):
    return pl.BlockSpec(shape, lambda i: (0,) * len(shape))


def gather(volt, cols, slots, tile):
    cells, nodes = volt.shape
    return pl.pallas_call(
        gather_kernel,
        grid=(slots // tile,),
        in_specs=[whole_block((cells, nodes)), pl.BlockSpec((tile, 4), lambda i: (i, 0))],
        out_specs=pl.BlockSpec((tile, LANES), lambda i: (i, 0)),
        out_shape=jax.ShapeDtypeStruct((slots, LANES), jnp.float32),
        scratch_shapes=[pltpu.VMEM((2 * cells, nodes), jnp.bfloat16)],
        compiler_params=params(),
    )(volt, cols)


def steklov(ident, volt, recov, templates):
    cells, nodes = volt.shape
    count = templates.shape[0]
    return pl.pallas_call(
        steklov_kernel,
        grid=(count,),
        in_specs=[
            whole_block((cells, 1)),
            whole_block((cells, nodes)),
            whole_block((cells, nodes)),
            pl.BlockSpec((1, nodes, nodes), lambda i: (i, 0, 0)),
        ],
        out_specs=whole_block((cells, nodes)),
        out_shape=jax.ShapeDtypeStruct((cells, nodes), jnp.float32),
        compiler_params=params(),
        cost_estimate=pl.CostEstimate(
            flops=2 * count * cells * nodes * nodes, bytes_accessed=2 * count * nodes * nodes, transcendentals=0
        ),
    )(ident, volt, recov, templates)


def scatter(got, sent, cols, conduct, cell_rows, base, memb, memb_t, grid_rows, tile):
    cells, nodes = base.shape
    slots = got.shape[0]
    return pl.pallas_call(
        scatter_kernel,
        grid=(slots // tile,),
        in_specs=[
            pl.BlockSpec((tile, LANES), lambda i: (i, 0)),
            pl.BlockSpec((tile, LANES), lambda i: (i, 0)),
            pl.BlockSpec((tile, 4), lambda i: (i, 0)),
            pl.BlockSpec((tile, 2), lambda i: (i, 0)),
            pl.BlockSpec((2, tile), lambda i: (0, i)),
            whole_block((cells, nodes)),
            whole_block(memb.shape),
            whole_block(memb_t.shape),
        ],
        out_specs=[whole_block((cells, nodes)), whole_block((grid_rows, LANES))],
        out_shape=[
            jax.ShapeDtypeStruct((cells, nodes), jnp.float32),
            jax.ShapeDtypeStruct((grid_rows, LANES), jnp.float32),
        ],
        scratch_shapes=[pltpu.VMEM((cells, nodes), jnp.float32)],
        compiler_params=params(),
    )(got, sent, cols, conduct, cell_rows, base, memb, memb_t)


def update(volt, recov, current, phi, memb):
    return pl.pallas_call(
        update_kernel,
        out_shape=[jax.ShapeDtypeStruct(volt.shape, jnp.float32)] * 2,
        compiler_params=params(),
    )(volt, recov, current, phi, memb)


def slot_table(patch_src, targets, patch_dst, patch_conduct, devices, capacity):
    patches = patch_src.shape[0]
    onehot = (targets[:, None] == jnp.arange(devices, dtype=jnp.int32)[None, :]).astype(jnp.int32)
    order = jnp.arange(patches, dtype=jnp.int32)
    earlier = (order[:, None] > order[None, :]).astype(jnp.bfloat16)
    before = dot32(earlier, onehot.astype(jnp.bfloat16))
    slot = jnp.sum(onehot * before.astype(jnp.int32), axis=1)
    position = targets * capacity + slot
    hit = (jnp.arange(devices * capacity, dtype=jnp.int32)[:, None] == position[None, :]).astype(jnp.bfloat16)
    first = lax.reduce_precision(patch_conduct, 8, 7)
    second = lax.reduce_precision(patch_conduct - first, 8, 7)
    third = patch_conduct - first - second
    values = [patch_src // BLOCK, patch_src % BLOCK, patch_dst // BLOCK, patch_dst % BLOCK]
    values = [v.astype(jnp.bfloat16) for v in values + [jnp.ones_like(patch_src), first, second, third]]
    table = dot32(hit, jnp.stack(values, axis=1))
    empty = table[:, 4] - 1.0
    src = table[:, 0] * BLOCK + table[:, 1] + empty
    dst = table[:, 2] * BLOCK + table[:, 3] + empty
    return src, dst, table[:, 5] + table[:, 6] + table[:, 7]


def exchange(x):
    return lax.all_to_all(x, ("tx", "ty"), split_axis=0, concat_axis=0, tiled=True)


def on_device(
    potential,
    gating,
    ecs_start,
    templates,
    template_id,
    patch_src,
    patch_dev,
    patch_dst,
    patch_conduct,
    memb_point,
):
    cells, nodes = potential.shape
    per_cell = nodes // BLOCK
    tile = ecs_start.shape[0]
    points = ecs_start.size
    count_x = lax.axis_size("tx")
    count_y = lax.axis_size("ty")
    devices = count_x * count_y
    patches = patch_src.shape[0]
    capacity = 2 * patches // devices
    slots = devices * capacity
    rows_at_once = min(512, slots)
    src, dst, conduct = slot_table(patch_src, patch_dev[:, 0], patch_dst, patch_conduct, devices, capacity)
    head = jnp.concatenate([dst.reshape(devices, capacity), conduct.reshape(devices, capacity)], axis=1)
    got_head = exchange(head)
    got_dst = got_head[:, :capacity].reshape(slots)
    got_conduct = got_head[:, capacity:].reshape(slots)
    places = []
    for patch in (src, got_dst):
        patch = patch.astype(jnp.int32)
        places += [jnp.where(patch < 0, -1, patch // per_cell), patch % per_cell]
    cols = jnp.stack(places, axis=1)
    cell_rows = jnp.stack([places[0], places[2]], axis=0)
    conduct_cols = jnp.stack([got_conduct, conduct], axis=1)
    memb = memb_point.reshape(cells, per_cell)
    memb_t = memb.T
    ident = template_id[:, None]
    start_x = lax.axis_index("tx") * tile
    start_y = lax.axis_index("ty") * tile
    volt = potential
    recov = gating
    phi = ecs_start
    for step in range(STEPS):
        sent = gather(volt, cols, slots, rows_at_once)
        got = exchange(sent.reshape(devices, capacity, LANES)).reshape(slots, LANES)
        base = steklov(ident, volt, recov, templates)
        current, deposit = scatter(
            got, sent, cols, conduct_cols, cell_rows, base, memb, memb_t, points // LANES, rows_at_once
        )
        deposit = deposit.reshape(ecs_start.shape)
        depth = SWEEPS
        framed_phi, framed_dep = (
            extended(phi, (("tx", 0), ("ty", 1)), depth),
            extended(deposit, (("tx", 0), ("ty", 1)), depth),
        )
        current_phi = framed_phi
        for sweep in range(SWEEPS):
            rim = depth - sweep - 1
            padded = jnp.pad(current_phi, ((0, 0), (0, 0), (1, 1)))
            total = stencil_sum(padded)
            lo = depth - rim
            hi = depth + tile + rim
            dep_crop = framed_dep[lo:hi, lo:hi, :]
            updated = (dep_crop + total) / 6.5
            span = jnp.arange(tile + 2 * rim, dtype=jnp.int32) - rim
            inside_x = (start_x + span >= 0) & (start_x + span < tile * count_x)
            inside_y = (start_y + span >= 0) & (start_y + span < tile * count_y)
            inside = inside_x[:, None, None] & inside_y[None, :, None]
            current_phi = jnp.where(inside, updated, 0.0)
        phi = current_phi
        volt, recov = update(volt, recov, current, phi.reshape(points // LANES, LANES), memb)
    return (volt, phi)


def solution(mesh):
    return jax.shard_map(
        on_device,
        mesh=mesh,
        in_specs=(
            P(("tx", "ty"), None),
            P(("tx", "ty"), None),
            P("tx", "ty", None),
            P(),
            P(("tx", "ty")),
            P(("tx", "ty")),
            P(("tx", "ty"), None),
            P(("tx", "ty")),
            P(("tx", "ty")),
            P(("tx", "ty")),
        ),
        out_specs=(P(("tx", "ty"), None), P("tx", "ty", None)),
        check_vma=False,
    )
```

profile of v0, /device:TPU:3, one launch (start us, length us, event | category | flops | bytes accessed | tf_op | source)
XLA Modules:
  0.0 195.0 jit_solution(9812621881747292240)
XLA Ops:
  8.5 6.4 %all-to-all-start = ((f32[32,1,128]{2,1,0:T(1,128)}), f32[32,1,128]{2,1,0:T(1,128)S(1)}, u32[]{:S(2)}, u32[]{:S(2)}) async-start(f32[32,1,128]{2,1,0:T(1,128)} %bitcast.2), calls=%async_computation | async-start | bytes 32768 | tf_op jit(solution)/shard_map/all_to_all | solution.py:264
  15.6 3.3 %collective-permute-start.4 = (f32[4,32,32]{2,1,0:T(8,128)}, f32[4,32,32]{2,1,0:T(8,128)}, u32[]{:S(2)}, u32[]{:S(2)}) collective-permute-start(f32[4,32,32]{2,1,0:T(8,128)} %get-tuple-element.33), channel_id=1, source_target_pairs={{0,4},{4,8},{8,12},{12,16},{16,20},{20,24},{24,28},{1,5},{5,9},{9,... | collective-permute-start | bytes 49160 | tf_op jit(solution)/shard_map/ppermute | solution.py:22
  19.0 1.9 collective-permute-start.5
  23.3 6.8 %shard_map.113.sent_ref = f32[2048,128]{1,0:T(8,128)} custom-call(f32[256,768]{1,0:T(8,128)S(1)} %copy-done.2, s32[2048,4]{1,0:T(8,128)S(1)} %copy.43.cols_ref), custom_call_target="tpu_custom_call" | custom-call | tf_op jit(solution)/shard_map/pallas_call | solution.py:176
  30.0 6.2 %all-to-all-start.1 = ((f32[32,64,128]{2,1,0:T(8,128)}), f32[32,64,128]{2,1,0:T(8,128)}, u32[]{:S(2)}, u32[]{:S(2)}) async-start(f32[32,64,128]{2,1,0:T(8,128)} %bitcast.4), calls=%async_computation.1 | async-start | bytes 2097152 | tf_op jit(solution)/shard_map/all_to_all | solution.py:264
  37.1 4.3 %copy-done = bf16[10,768,768]{2,1,0:T(8,128)(2,1)S(1)} copy-done((bf16[10,768,768]{2,1,0:T(8,128)(2,1)S(1)}, bf16[10,768,768]{2,1,0:T(8,128)(2,1)}, u32[]{:S(2)}) %copy-start) | copy-done | bytes 11796504
  41.4 5.9 %shard_map.114.base_ref = f32[256,768]{1,0:T(8,128)S(1)} custom-call(s32[256,1]{1,0:T(8,128)S(1)} %copy.44.ident_ref, f32[256,768]{1,0:T(8,128)S(1)} %copy-done.2, f32[256,768]{1,0:T(8,128)S(1)} %copy-done.8, bf16[10,768,768]{2,1,0:T(8,128)(2,1)S(1)} %copy-done), custom_call_target="tpu_custom_call" | custom-call | flops 3019898880 | bytes 11796480 | tf_op jit(solution)/shard_map/pallas_call | solution.py:190
  52.9 9.6 %all-to-all-done.1 = f32[32,64,128]{2,1,0:T(8,128)} async-done(((f32[32,64,128]{2,1,0:T(8,128)}), f32[32,64,128]{2,1,0:T(8,128)}, u32[]{:S(2)}, u32[]{:S(2)}) %all-to-all-start.1) | async-done | bytes 1048608 | tf_op jit(solution)/shard_map/all_to_all | solution.py:264
  63.6 10.6 %shard_map.115 = (f32[256,768]{1,0:T(8,128)S(1)}, f32[256,128]{1,0:T(8,128)S(1)}) custom-call(f32[2048,128]{1,0:T(8,128)} %bitcast.5.got_ref, f32[2048,128]{1,0:T(8,128)} %shard_map.113.sent_ref, s32[2048,4]{1,0:T(8,128)S(1)} %copy.43.cols_ref, f32[2048,2]{1,0:T(8,128)S(1)} %copy.47.conduct_ref, s32[2,2048]{1,0:T(2,128)S(1)} %pad_add_fusion.1.cells_ref, ...), custom_call_target="tpu_custom_call" | custom-call | tf_op jit(solution)/shard_map/pallas_call | solution.py:211
  76.4 1.9 collective-permute-start
  78.3 1.7 fusion.68
  80.0 3.8 %collective-permute-start.6 = (f32[40,4,32]{2,1,0:T(4,128)}, f32[40,4,32]{2,1,0:T(4,128)S(1)}, u32[]{:S(2)}, u32[]{:S(2)}) collective-permute-start(f32[40,4,32]{2,1,0:T(4,128)} %get-tuple-element.28), channel_id=1, source_target_pairs={{0,1},{1,2},{2,3},{4,5},{5,6},{6,7},{8,9},{9,10},{10,11},{12,13},{... | collective-permute-start | bytes 61448 | tf_op jit(solution)/shard_map/ppermute | solution.py:22
  86.8 2.0 %collective-permute-start.1 = (f32[4,32,32]{2,1,0:T(8,128)S(1)}, f32[4,32,32]{2,1,0:T(8,128)S(1)}, u32[]{:S(2)}, u32[]{:S(2)}) collective-permute-start(f32[4,32,32]{2,1,0:T(8,128)S(1)} %slice.297), channel_id=1, source_target_pairs={{4,0},{8,4},{12,8},{16,12},{20,16},{24,20},{28,24},{5,1},{9,5},{13... | collective-permute-start | bytes 49160 | tf_op jit(solution)/shard_map/ppermute | solution.py:23
  90.8 2.6 %collective-permute-done.1 = f32[4,32,32]{2,1,0:T(8,128)S(1)} collective-permute-done((f32[4,32,32]{2,1,0:T(8,128)S(1)}, f32[4,32,32]{2,1,0:T(8,128)S(1)}, u32[]{:S(2)}, u32[]{:S(2)}) %collective-permute-start.1) | collective-permute-done | bytes 16416 | tf_op jit(solution)/shard_map/ppermute | solution.py:23
  93.5 4.0 %collective-permute-start.2 = (f32[40,4,32]{2,1,0:T(4,128)S(1)}, f32[40,4,32]{2,1,0:T(4,128)S(1)}, u32[]{:S(2)}, u32[]{:S(2)}) collective-permute-start(f32[40,4,32]{2,1,0:T(4,128)S(1)} %get-tuple-element.26), channel_id=1, source_target_pairs={{0,1},{1,2},{2,3},{4,5},{5,6},{6,7},{8,9},{9,10},{10,11},{12,13},{... | collective-permute-start | bytes 61448 | tf_op jit(solution)/shard_map/ppermute | solution.py:22
  100.2 2.5 %collective-permute-done.3 = f32[40,4,32]{2,1,0:T(4,128)S(1)} collective-permute-done((f32[40,4,32]{2,1,0:T(4,128)S(1)}, f32[40,4,32]{2,1,0:T(4,128)S(1)}, u32[]{:S(2)}, u32[]{:S(2)}) %collective-permute-start.3) | collective-permute-done | bytes 20512 | tf_op jit(solution)/shard_map/ppermute | solution.py:23
  109.6 3.5 %shard_map.116 = (f32[256,768]{1,0:T(8,128)S(1)}, f32[256,768]{1,0:T(8,128)S(1)}) custom-call(f32[256,768]{1,0:T(8,128)S(1)} %copy-done.2, f32[256,768]{1,0:T(8,128)S(1)} %copy-done.9, f32[256,768]{1,0:T(8,128)S(1)} %copy-done.16, f32[256,128]{1,0:T(8,128)S(1)} %reshape.448.phi_ref, s32[256,12]{1,0:T(8,128)S(1)} %reshape.446.memb_ref), custom_call_target="tpu_custom_call" | custom-call | tf_op jit(solution)/shard_map/pallas_call | solution.py:235
  113.1 6.8 %shard_map.117.sent_ref = f32[2048,128]{1,0:T(8,128)} custom-call(f32[256,768]{1,0:T(8,128)S(1)} %get-tuple-element.11.volt_ref, s32[2048,4]{1,0:T(8,128)S(1)} %copy.43.cols_ref), custom_call_target="tpu_custom_call" | custom-call | tf_op jit(solution)/shard_map/pallas_call | solution.py:176
  120.7 3.3 %all-to-all-start.2 = ((f32[32,64,128]{2,1,0:T(8,128)}), f32[32,64,128]{2,1,0:T(8,128)}, u32[]{:S(2)}, u32[]{:S(2)}) async-start(f32[32,64,128]{2,1,0:T(8,128)} %bitcast.11), calls=%async_computation.2 | async-start | bytes 2097152 | tf_op jit(solution)/shard_map/all_to_all | solution.py:264
  124.9 3.3 %collective-permute-start.12 = (f32[4,32,32]{2,1,0:T(8,128)S(1)}, f32[4,32,32]{2,1,0:T(8,128)S(1)}, u32[]{:S(2)}, u32[]{:S(2)}) collective-permute-start(f32[4,32,32]{2,1,0:T(8,128)S(1)} %get-tuple-element.30), channel_id=1, source_target_pairs={{0,4},{4,8},{8,12},{12,16},{16,20},{20,24},{24,28},{1,5},{5,9},{9,... | collective-permute-start | bytes 49160 | tf_op jit(solution)/shard_map/ppermute | solution.py:22
  128.2 1.9 collective-permute-start.13
  130.2 4.3 %copy-done.1 = bf16[10,768,768]{2,1,0:T(8,128)(2,1)S(1)} copy-done((bf16[10,768,768]{2,1,0:T(8,128)(2,1)S(1)}, bf16[10,768,768]{2,1,0:T(8,128)(2,1)}, u32[]{:S(2)}) %copy-start.1) | copy-done | bytes 11796504
  136.8 5.9 %shard_map.118.base_ref = f32[256,768]{1,0:T(8,128)S(1)} custom-call(s32[256,1]{1,0:T(8,128)S(1)} %copy.44.ident_ref, f32[256,768]{1,0:T(8,128)S(1)} %copy-done.4, f32[256,768]{1,0:T(8,128)S(1)} %copy-done.11, bf16[10,768,768]{2,1,0:T(8,128)(2,1)S(1)} %copy-done.1), custom_call_target="tpu_custom_call" | custom-call | flops 3019898880 | bytes 11796480 | tf_op jit(solution)/shard_map/pallas_call | solution.py:190
  142.7 7.5 %all-to-all-done.2 = f32[32,64,128]{2,1,0:T(8,128)} async-done(((f32[32,64,128]{2,1,0:T(8,128)}), f32[32,64,128]{2,1,0:T(8,128)}, u32[]{:S(2)}, u32[]{:S(2)}) %all-to-all-start.2) | async-done | bytes 1048608 | tf_op jit(solution)/shard_map/all_to_all | solution.py:264
  150.2 10.6 %shard_map.119 = (f32[256,768]{1,0:T(8,128)S(1)}, f32[256,128]{1,0:T(8,128)S(1)}) custom-call(f32[2048,128]{1,0:T(8,128)} %bitcast.12.got_ref, f32[2048,128]{1,0:T(8,128)} %shard_map.117.sent_ref, s32[2048,4]{1,0:T(8,128)S(1)} %copy.43.cols_ref, f32[2048,2]{1,0:T(8,128)S(1)} %copy.47.conduct_ref, s32[2,2048]{1,0:T(2,128)S(1)} %pad_add_fusion.1.cells_ref, ...), custom_call_target="tpu_custom_call" | custom-call | tf_op jit(solution)/shard_map/pallas_call | solution.py:211
  161.8 1.9 collective-permute-start.8
  164.8 3.8 %collective-permute-start.14 = (f32[40,4,32]{2,1,0:T(4,128)S(1)}, f32[40,4,32]{2,1,0:T(4,128)S(1)}, u32[]{:S(2)}, u32[]{:S(2)}) collective-permute-start(f32[40,4,32]{2,1,0:T(4,128)S(1)} %get-tuple-element.24), channel_id=1, source_target_pairs={{0,1},{1,2},{2,3},{4,5},{5,6},{6,7},{8,9},{9,10},{10,11},{12,13},{... | collective-permute-start | bytes 61448 | tf_op jit(solution)/shard_map/ppermute | solution.py:22
  170.1 1.9 collective-permute-start.9
  172.1 4.5 %collective-permute-done.9 = f32[4,32,32]{2,1,0:T(8,128)S(1)} collective-permute-done((f32[4,32,32]{2,1,0:T(8,128)S(1)}, f32[4,32,32]{2,1,0:T(8,128)S(1)}, u32[]{:S(2)}, u32[]{:S(2)}) %collective-permute-start.9) | collective-permute-done | bytes 16416 | tf_op jit(solution)/shard_map/ppermute | solution.py:23
  176.6 4.0 %collective-permute-start.10 = (f32[40,4,32]{2,1,0:T(4,128)S(1)}, f32[40,4,32]{2,1,0:T(4,128)S(1)}, u32[]{:S(2)}, u32[]{:S(2)}) collective-permute-start(f32[40,4,32]{2,1,0:T(4,128)S(1)} %get-tuple-element.22), channel_id=1, source_target_pairs={{0,1},{1,2},{2,3},{4,5},{5,6},{6,7},{8,9},{9,10},{10,11},{12,13},{... | collective-permute-start | bytes 61448 | tf_op jit(solution)/shard_map/ppermute | solution.py:22
  183.4 2.5 %collective-permute-done.11 = f32[40,4,32]{2,1,0:T(4,128)S(1)} collective-permute-done((f32[40,4,32]{2,1,0:T(4,128)S(1)}, f32[40,4,32]{2,1,0:T(4,128)S(1)}, u32[]{:S(2)}, u32[]{:S(2)}) %collective-permute-start.11) | collective-permute-done | bytes 20512 | tf_op jit(solution)/shard_map/ppermute | solution.py:23
  190.5 4.5 %shard_map.120 = (f32[256,768]{1,0:T(8,128)}, f32[256,768]{1,0:T(8,128)}) custom-call(f32[256,768]{1,0:T(8,128)S(1)} %copy-done.5, f32[256,768]{1,0:T(8,128)S(1)} %copy-done.12, f32[256,768]{1,0:T(8,128)S(1)} %copy-done.14, f32[256,128]{1,0:T(8,128)S(1)} %reshape.452.phi_ref, s32[256,12]{1,0:T(8,128)S(1)} %reshape.446.memb_ref), custom_call_target="tpu_custom_call" | custom-call | tf_op jit(solution)/shard_map/pallas_call | solution.py:235
  (155 shorter events, 49.9 us)
Async XLA Ops:
  0.6 14.3 %copy-start.18 = (f32[32,32,32]{2,1,0:T(8,128)S(1)}, f32[32,32,32]{2,1,0:T(8,128)}, u32[]{:S(2)}) copy-start(f32[32,32,32]{2,1,0:T(8,128)} %param.12) | copy-start | bytes 393220
  0.6 22.6 %copy-start.2 = (f32[256,768]{1,0:T(8,128)S(1)}, f32[256,768]{1,0:T(8,128)}, u32[]{:S(2)}) copy-start(f32[256,768]{1,0:T(8,128)} %volt_ref.5) | copy-start | bytes 2359300
  6.4 29.8 %copy-start.26 = (s32[256]{0:T(256)S(1)}, s32[256]{0:T(256)}, u32[]{:S(2)}) copy-start(s32[256]{0:T(256)} %param.14) | copy-start | bytes 3076
  6.5 30.6 %copy-start.8 = (f32[256,768]{1,0:T(8,128)S(1)}, f32[256,768]{1,0:T(8,128)}, u32[]{:S(2)}) copy-start(f32[256,768]{1,0:T(8,128)} %recov_ref.3) | copy-start | bytes 2359300
  8.5 13.8 %all-to-all-start = ((f32[32,1,128]{2,1,0:T(1,128)}), f32[32,1,128]{2,1,0:T(1,128)S(1)}, u32[]{:S(2)}, u32[]{:S(2)}) async-start(f32[32,1,128]{2,1,0:T(1,128)} %bitcast.2), calls=%async_computation | async-start | bytes 32768 | tf_op jit(solution)/shard_map/all_to_all | solution.py:264
  15.6 33.5 %collective-permute-start.4 = (f32[4,32,32]{2,1,0:T(8,128)}, f32[4,32,32]{2,1,0:T(8,128)}, u32[]{:S(2)}, u32[]{:S(2)}) collective-permute-start(f32[4,32,32]{2,1,0:T(8,128)} %get-tuple-element.33), channel_id=1, source_target_pairs={{0,4},{4,8},{8,12},{12,16},{16,20},{20,24},{24,28},{1,5},{5,9},{9,... | collective-permute-start | bytes 49160 | tf_op jit(solution)/shard_map/ppermute | solution.py:22
  19.0 32.4 %collective-permute-start.5 = (f32[4,32,32]{2,1,0:T(8,128)}, f32[4,32,32]{2,1,0:T(8,128)S(1)}, u32[]{:S(2)}, u32[]{:S(2)}) collective-permute-start(f32[4,32,32]{2,1,0:T(8,128)} %get-tuple-element.32), channel_id=1, source_target_pairs={{4,0},{8,4},{12,8},{16,12},{20,16},{24,20},{28,24},{5,1},{9,5},{13... | collective-permute-start | bytes 49160 | tf_op jit(solution)/shard_map/ppermute | solution.py:23
  30.0 32.4 %all-to-all-start.1 = ((f32[32,64,128]{2,1,0:T(8,128)}), f32[32,64,128]{2,1,0:T(8,128)}, u32[]{:S(2)}, u32[]{:S(2)}) async-start(f32[32,64,128]{2,1,0:T(8,128)} %bitcast.4), calls=%async_computation.1 | async-start | bytes 2097152 | tf_op jit(solution)/shard_map/all_to_all | solution.py:264
  37.1 4.4 %copy-start = (bf16[10,768,768]{2,1,0:T(8,128)(2,1)S(1)}, bf16[10,768,768]{2,1,0:T(8,128)(2,1)}, u32[]{:S(2)}) copy-start(bf16[10,768,768]{2,1,0:T(8,128)(2,1)} %template_ref.3) | copy-start | bytes 35389444
  41.4 7.4 %copy-start.25 = (s32[3072]{0:T(1024)S(1)}, s32[3072]{0:T(1024)}, u32[]{:S(2)}) copy-start(s32[3072]{0:T(1024)} %param.19) | copy-start | bytes 36868
  76.4 12.5 %collective-permute-start = (f32[4,32,32]{2,1,0:T(8,128)}, f32[4,32,32]{2,1,0:T(8,128)}, u32[]{:S(2)}, u32[]{:S(2)}) collective-permute-start(f32[4,32,32]{2,1,0:T(8,128)} %slice.295), channel_id=1, source_target_pairs={{0,4},{4,8},{8,12},{12,16},{16,20},{20,24},{24,28},{1,5},{5,9},{9,... | collective-permute-start | bytes 49160 | tf_op jit(solution)/shard_map/ppermute | solution.py:22
  80.0 19.0 %collective-permute-start.6 = (f32[40,4,32]{2,1,0:T(4,128)}, f32[40,4,32]{2,1,0:T(4,128)S(1)}, u32[]{:S(2)}, u32[]{:S(2)}) collective-permute-start(f32[40,4,32]{2,1,0:T(4,128)} %get-tuple-element.28), channel_id=1, source_target_pairs={{0,1},{1,2},{2,3},{4,5},{5,6},{6,7},{8,9},{9,10},{10,11},{12,13},{... | collective-permute-start | bytes 61448 | tf_op jit(solution)/shard_map/ppermute | solution.py:22
  83.8 15.2 %collective-permute-start.7 = (f32[40,4,32]{2,1,0:T(4,128)S(1)}, f32[40,4,32]{2,1,0:T(4,128)S(1)}, u32[]{:S(2)}, u32[]{:S(2)}) collective-permute-start(f32[40,4,32]{2,1,0:T(4,128)S(1)} %get-tuple-element.29), channel_id=1, source_target_pairs={{1,0},{2,1},{3,2},{5,4},{6,5},{7,6},{9,8},{10,9},{11,10},{13,12},{... | collective-permute-start | bytes 61448 | tf_op jit(solution)/shard_map/ppermute | solution.py:23
  86.8 16.0 %copy-start.19 = (pred[38,38]{1,0:T(8,128)(4,1)S(1)}, pred[38,38]{1,0:T(8,128)(4,1)}, u32[]{:S(2)}) copy-start(pred[38,38]{1,0:T(8,128)(4,1)} %broadcast_and_fusion) | copy-start | bytes 4336
  86.8 6.6 %collective-permute-start.1 = (f32[4,32,32]{2,1,0:T(8,128)S(1)}, f32[4,32,32]{2,1,0:T(8,128)S(1)}, u32[]{:S(2)}, u32[]{:S(2)}) collective-permute-start(f32[4,32,32]{2,1,0:T(8,128)S(1)} %slice.297), channel_id=1, source_target_pairs={{4,0},{8,4},{12,8},{16,12},{20,16},{24,20},{28,24},{5,1},{9,5},{13... | collective-permute-start | bytes 49160 | tf_op jit(solution)/shard_map/ppermute | solution.py:23
  93.5 6.7 %collective-permute-start.2 = (f32[40,4,32]{2,1,0:T(4,128)S(1)}, f32[40,4,32]{2,1,0:T(4,128)S(1)}, u32[]{:S(2)}, u32[]{:S(2)}) collective-permute-start(f32[40,4,32]{2,1,0:T(4,128)S(1)} %get-tuple-element.26), channel_id=1, source_target_pairs={{0,1},{1,2},{2,3},{4,5},{5,6},{6,7},{8,9},{9,10},{10,11},{12,13},{... | collective-permute-start | bytes 61448 | tf_op jit(solution)/shard_map/ppermute | solution.py:22
  97.5 6.0 %copy-start.21 = (pred[36,36]{1,0:T(8,128)(4,1)S(1)}, pred[36,36]{1,0:T(8,128)(4,1)}, u32[]{:S(2)}) copy-start(pred[36,36]{1,0:T(8,128)(4,1)} %broadcast_and_fusion.1) | copy-start | bytes 3892
  97.5 5.2 %collective-permute-start.3 = (f32[40,4,32]{2,1,0:T(4,128)S(1)}, f32[40,4,32]{2,1,0:T(4,128)S(1)}, u32[]{:S(2)}, u32[]{:S(2)}) collective-permute-start(f32[40,4,32]{2,1,0:T(4,128)S(1)} %get-tuple-element.27), channel_id=1, source_target_pairs={{1,0},{2,1},{3,2},{5,4},{6,5},{7,6},{9,8},{10,9},{11,10},{13,12},{... | collective-permute-start | bytes 61448 | tf_op jit(solution)/shard_map/ppermute | solution.py:23
  113.1 6.8 %copy-start.10 = (f32[256,768]{1,0:T(8,128)}, f32[256,768]{1,0:T(8,128)S(1)}, u32[]{:S(2)}) copy-start(f32[256,768]{1,0:T(8,128)S(1)} %get-tuple-element.12.recov_ref) | copy-start | bytes 2359300
  120.7 29.5 %all-to-all-start.2 = ((f32[32,64,128]{2,1,0:T(8,128)}), f32[32,64,128]{2,1,0:T(8,128)}, u32[]{:S(2)}, u32[]{:S(2)}) async-start(f32[32,64,128]{2,1,0:T(8,128)} %bitcast.11), calls=%async_computation.2 | async-start | bytes 2097152 | tf_op jit(solution)/shard_map/all_to_all | solution.py:264
  124.9 38.9 %collective-permute-start.12 = (f32[4,32,32]{2,1,0:T(8,128)S(1)}, f32[4,32,32]{2,1,0:T(8,128)S(1)}, u32[]{:S(2)}, u32[]{:S(2)}) collective-permute-start(f32[4,32,32]{2,1,0:T(8,128)S(1)} %get-tuple-element.30), channel_id=1, source_target_pairs={{0,4},{4,8},{8,12},{12,16},{16,20},{20,24},{24,28},{1,5},{5,9},{9,... | collective-permute-start | bytes 49160 | tf_op jit(solution)/shard_map/ppermute | solution.py:22
  128.2 35.5 %collective-permute-start.13 = (f32[4,32,32]{2,1,0:T(8,128)S(1)}, f32[4,32,32]{2,1,0:T(8,128)S(1)}, u32[]{:S(2)}, u32[]{:S(2)}) collective-permute-start(f32[4,32,32]{2,1,0:T(8,128)S(1)} %get-tuple-element.31), channel_id=1, source_target_pairs={{4,0},{8,4},{12,8},{16,12},{20,16},{24,20},{28,24},{5,1},{9,5},{13... | collective-permute-start | bytes 49160 | tf_op jit(solution)/shard_map/ppermute | solution.py:23
  130.2 4.4 %copy-start.1 = (bf16[10,768,768]{2,1,0:T(8,128)(2,1)S(1)}, bf16[10,768,768]{2,1,0:T(8,128)(2,1)}, u32[]{:S(2)}) copy-start(bf16[10,768,768]{2,1,0:T(8,128)(2,1)} %template_ref.3) | copy-start | bytes 35389444
  161.7 24.2 %copy-start.20 = (pred[38,38]{1,0:T(8,128)(4,1)S(1)}, pred[38,38]{1,0:T(8,128)(4,1)}, u32[]{:S(2)}) copy-start(pred[38,38]{1,0:T(8,128)(4,1)} %broadcast_and_fusion) | copy-start | bytes 4336
  161.8 10.2 %collective-permute-start.8 = (f32[4,32,32]{2,1,0:T(8,128)S(1)}, f32[4,32,32]{2,1,0:T(8,128)S(1)}, u32[]{:S(2)}, u32[]{:S(2)}) collective-permute-start(f32[4,32,32]{2,1,0:T(8,128)S(1)} %slice.332), channel_id=1, source_target_pairs={{0,4},{4,8},{8,12},{12,16},{16,20},{20,24},{24,28},{1,5},{5,9},{9,... | collective-permute-start | bytes 49160 | tf_op jit(solution)/shard_map/ppermute | solution.py:22
  164.8 17.4 %collective-permute-start.14 = (f32[40,4,32]{2,1,0:T(4,128)S(1)}, f32[40,4,32]{2,1,0:T(4,128)S(1)}, u32[]{:S(2)}, u32[]{:S(2)}) collective-permute-start(f32[40,4,32]{2,1,0:T(4,128)S(1)} %get-tuple-element.24), channel_id=1, source_target_pairs={{0,1},{1,2},{2,3},{4,5},{5,6},{6,7},{8,9},{9,10},{10,11},{12,13},{... | collective-permute-start | bytes 61448 | tf_op jit(solution)/shard_map/ppermute | solution.py:22
  168.6 13.6 %collective-permute-start.15 = (f32[40,4,32]{2,1,0:T(4,128)S(1)}, f32[40,4,32]{2,1,0:T(4,128)S(1)}, u32[]{:S(2)}, u32[]{:S(2)}) collective-permute-start(f32[40,4,32]{2,1,0:T(4,128)S(1)} %get-tuple-element.25), channel_id=1, source_target_pairs={{1,0},{2,1},{3,2},{5,4},{6,5},{7,6},{9,8},{10,9},{11,10},{13,12},{... | collective-permute-start | bytes 61448 | tf_op jit(solution)/shard_map/ppermute | solution.py:23
  170.1 6.5 %collective-permute-start.9 = (f32[4,32,32]{2,1,0:T(8,128)S(1)}, f32[4,32,32]{2,1,0:T(8,128)S(1)}, u32[]{:S(2)}, u32[]{:S(2)}) collective-permute-start(f32[4,32,32]{2,1,0:T(8,128)S(1)} %slice.334), channel_id=1, source_target_pairs={{4,0},{8,4},{12,8},{16,12},{20,16},{24,20},{28,24},{5,1},{9,5},{13... | collective-permute-start | bytes 49160 | tf_op jit(solution)/shard_map/ppermute | solution.py:23
  176.6 6.7 %collective-permute-start.10 = (f32[40,4,32]{2,1,0:T(4,128)S(1)}, f32[40,4,32]{2,1,0:T(4,128)S(1)}, u32[]{:S(2)}, u32[]{:S(2)}) collective-permute-start(f32[40,4,32]{2,1,0:T(4,128)S(1)} %get-tuple-element.22), channel_id=1, source_target_pairs={{0,1},{1,2},{2,3},{4,5},{5,6},{6,7},{8,9},{9,10},{10,11},{12,13},{... | collective-permute-start | bytes 61448 | tf_op jit(solution)/shard_map/ppermute | solution.py:22
  180.6 6.0 %copy-start.22 = (pred[36,36]{1,0:T(8,128)(4,1)S(1)}, pred[36,36]{1,0:T(8,128)(4,1)}, u32[]{:S(2)}) copy-start(pred[36,36]{1,0:T(8,128)(4,1)} %broadcast_and_fusion.1) | copy-start | bytes 3892
  180.7 5.2 %collective-permute-start.11 = (f32[40,4,32]{2,1,0:T(4,128)S(1)}, f32[40,4,32]{2,1,0:T(4,128)S(1)}, u32[]{:S(2)}, u32[]{:S(2)}) collective-permute-start(f32[40,4,32]{2,1,0:T(4,128)S(1)} %get-tuple-element.23), channel_id=1, source_target_pairs={{1,0},{2,1},{3,2},{5,4},{6,5},{7,6},{9,8},{10,9},{11,10},{13,12},{... | collective-permute-start | bytes 61448 | tf_op jit(solution)/shard_map/ppermute | solution.py:23
  187.3 3.2 %copy-start.5 = (f32[256,768]{1,0:T(8,128)S(1)}, f32[256,768]{1,0:T(8,128)}, u32[]{:S(2)}) copy-start(f32[256,768]{1,0:T(8,128)} %copy-done.3) | copy-start | bytes 2359300
  (14 other events, 19.6 us)
where the time goes:
time: 197 us; the launch traced here: 195 us
  starting transfers between devices  55.3 us (28%)
  Pallas kernels  54.4 us (28%)
  local copies, waits for them, and re-layouts  34.5 us (18%)
  waiting for transfers between devices  29.2 us (15%)
  other arithmetic  17.4 us (9%)
  matrix products  2.76 us (1%)
    ppermute x8, starting transfers between devices, extended(): before = lax.ppermute(last, axis, up)  26.1 us
    unnamed x60, local copies, waits for them, and re-layouts  22.2 us
    pallas_call x2, Pallas kernels, scatter(): pl.pallas_call(scatter_kernel, grid=(slots // tile,), in_specs=[pl.BlockS...  21.2 us
    all_to_all x3, waiting for transfers between devices, exchange(): lax.all_to_all(x, ('tx', 'ty'), split_axis=0, concat_axis=0, tiled=True)  17.1 us
    all_to_all x3, starting transfers between devices, exchange(): lax.all_to_all(x, ('tx', 'ty'), split_axis=0, concat_axis=0, tiled=True)  15.9 us
    pallas_call x2, Pallas kernels, gather(): pl.pallas_call(gather_kernel, grid=(slots // tile,), in_specs=[whole_bloc...  13.5 us
    ppermute x8, starting transfers between devices, extended(): after = lax.ppermute(leading, axis, down)  13.4 us
    ppermute x8, waiting for transfers between devices, extended(): after = lax.ppermute(leading, axis, down)  12 us
  transfers between devices with their start and end apart: 19, of which 6 were waited for; matrix products, arithmetic and copies ran while one was open for 9% of the time, Pallas kernels for 15%

commit v1 on v0

--- a/solution.py
+++ b/solution.py
@@ -1,3 +1,5 @@
+import functools
+
 import jax
 import jax.numpy as jnp
 from jax import lax
@@ -89,7 +91,19 @@
 
 
 def scatter_kernel(
-    got_ref, sent_ref, cols_ref, conduct_ref, cells_ref, base_ref, memb_ref, memb_t_ref, current_ref, deposit_ref, gap_ref
+    got_ref,
+    sent_ref,
+    shift_ref,
+    cols_ref,
+    conduct_ref,
+    cells_ref,
+    base_ref,
+    volt_ref,
+    memb_ref,
+    memb_t_ref,
+    early_ref,
+    deposit_ref,
+    gap_ref,
 ):
     cells, nodes = base_ref.shape
     rows = got_ref.shape[0]
@@ -103,7 +117,8 @@
     cols = cols_ref[...]
     conduct = conduct_ref[...]
     scale = jnp.where(lane < BLOCK, conduct[:, 0:1], conduct[:, 1:2])
-    flux = scale * (got_ref[...] - pltpu.roll(sent_ref[...], BLOCK, 1))
+    shift = jnp.where(lane < BLOCK, shift_ref[:, 0:1], shift_ref[:, 1:2])
+    flux = scale * (got_ref[...] - pltpu.roll(sent_ref[...], BLOCK, 1) - shift)
     turned = pltpu.roll(flux, BLOCK, 1)
     own_row = lax.broadcasted_iota(jnp.int32, (cells, rows), 0)
 
@@ -124,7 +139,7 @@
     @pl.when(pl.program_id(0) == pl.num_programs(0) - 1)
     def _():
         current = base_ref[...] - gap_ref[...]
-        current_ref[...] = current
+        early_ref[...] = volt_ref[...] - 0.05 * current
         grid_rows = deposit_ref.shape[0]
         grid_row = lax.broadcasted_iota(jnp.int32, (grid_rows, cells), 0)
         cell_lane = lax.broadcasted_iota(jnp.int32, (cells, LANES), 1)
@@ -141,7 +156,7 @@
         deposit_ref[...] = total
 
 
-def update_kernel(volt_ref, recov_ref, current_ref, phi_ref, memb_ref, volt_out, recov_out):
+def update_kernel(volt_ref, recov_ref, early_ref, phi_ref, memb_ref, volt_out, recov_out, phi_t_ref):
     cells, nodes = volt_ref.shape
     grid_rows = phi_ref.shape[0]
     high, low = two_parts(phi_ref[...])
@@ -155,12 +170,29 @@
         row = dot32(jnp.concatenate([hit, hit], axis=1), both)
         return jnp.sum(jnp.where(lane == (memb & (LANES - 1)), row, 0.0), axis=1, keepdims=True)
 
+    table = jnp.zeros((cells, LANES), jnp.float32)
     for g in range(nodes // LANES):
-        phi_nodes = jnp.where(lane < BLOCK, value(2 * g), value(2 * g + 1))
+        first, second = value(2 * g), value(2 * g + 1)
+        table = jnp.where(lane == 2 * g, first, jnp.where(lane == 2 * g + 1, second, table))
         span = slice(g * LANES, (g + 1) * LANES)
         volt, recov = volt_ref[:, span], recov_ref[:, span]
         recov_out[:, span] = recov + 0.05 * 0.08 * (volt + 0.7 - 0.8 * recov)
-        volt_out[:, span] = volt - 0.05 * (current_ref[:, span] + phi_nodes)
+        volt_out[:, span] = early_ref[:, span] - 0.05 * jnp.where(lane < BLOCK, first, second)
+    phi_t_ref[...] = table.T
+
+
+def slot_phi_kernel(kept, phi_t_ref, cells_ref, spots_ref, out_ref):
+    cells = phi_t_ref.shape[1]
+    slots = cells_ref.shape[1]
+    high, low = two_parts(phi_t_ref[0:kept, :])
+    both = jnp.concatenate([high, low], axis=1)
+    row_of = lax.broadcasted_iota(jnp.int32, (cells, slots), 0)
+    spot_of = lax.broadcasted_iota(jnp.int32, (kept, slots), 0)
+    for part in range(2):
+        hit = onehot_of(row_of == cells_ref[part : part + 1, :])
+        found = dot32(both, jnp.concatenate([hit, hit], axis=0))
+        kept_rows = jnp.where(spot_of == spots_ref[part : part + 1, :], found, 0.0)
+        out_ref[part : part + 1, :] = jnp.sum(kept_rows, axis=0, keepdims=True)
 
 
 def params():
@@ -198,14 +230,14 @@
         ],
         out_specs=whole_block((cells, nodes)),
         out_shape=jax.ShapeDtypeStruct((cells, nodes), jnp.float32),
-        compiler_params=params(),
+        compiler_params=pltpu.CompilerParams(vmem_limit_bytes=56 * 1024 * 1024),
         cost_estimate=pl.CostEstimate(
             flops=2 * count * cells * nodes * nodes, bytes_accessed=2 * count * nodes * nodes, transcendentals=0
         ),
     )(ident, volt, recov, templates)
 
 
-def scatter(got, sent, cols, conduct, cell_rows, base, memb, memb_t, grid_rows, tile):
+def scatter(got, sent, shift, cols, conduct, cell_rows, base, volt, memb, memb_t, grid_rows, tile):
     cells, nodes = base.shape
     slots = got.shape[0]
     return pl.pallas_call(
@@ -214,9 +246,11 @@
         in_specs=[
             pl.BlockSpec((tile, LANES), lambda i: (i, 0)),
             pl.BlockSpec((tile, LANES), lambda i: (i, 0)),
+            pl.BlockSpec((tile, 2), lambda i: (i, 0)),
             pl.BlockSpec((tile, 4), lambda i: (i, 0)),
             pl.BlockSpec((tile, 2), lambda i: (i, 0)),
             pl.BlockSpec((2, tile), lambda i: (0, i)),
+            whole_block((cells, nodes)),
             whole_block((cells, nodes)),
             whole_block(memb.shape),
             whole_block(memb_t.shape),
@@ -228,15 +262,24 @@
         ],
         scratch_shapes=[pltpu.VMEM((cells, nodes), jnp.float32)],
         compiler_params=params(),
-    )(got, sent, cols, conduct, cell_rows, base, memb, memb_t)
-
-
-def update(volt, recov, current, phi, memb):
+    )(got, sent, shift, cols, conduct, cell_rows, base, volt, memb, memb_t)
+
+
+def update(volt, recov, early, phi, memb):
+    arrays = [volt.shape, volt.shape, (LANES, volt.shape[0])]
     return pl.pallas_call(
         update_kernel,
-        out_shape=[jax.ShapeDtypeStruct(volt.shape, jnp.float32)] * 2,
+        out_shape=[jax.ShapeDtypeStruct(shape, jnp.float32) for shape in arrays],
         compiler_params=params(),
-    )(volt, recov, current, phi, memb)
+    )(volt, recov, early, phi, memb)
+
+
+def slot_phi(phi_t, cell_rows, spot_rows, per_cell):
+    return pl.pallas_call(
+        functools.partial(slot_phi_kernel, -(-per_cell // 16) * 16),
+        out_shape=jax.ShapeDtypeStruct(cell_rows.shape, jnp.float32),
+        compiler_params=params(),
+    )(phi_t, cell_rows, spot_rows)
 
 
 def slot_table(patch_src, targets, patch_dst, patch_conduct, devices, capacity):
@@ -298,6 +341,7 @@
         places += [jnp.where(patch < 0, -1, patch // per_cell), patch % per_cell]
     cols = jnp.stack(places, axis=1)
     cell_rows = jnp.stack([places[0], places[2]], axis=0)
+    spot_rows = jnp.stack([places[1], places[3]], axis=0)
     conduct_cols = jnp.stack([got_conduct, conduct], axis=1)
     memb = memb_point.reshape(cells, per_cell)
     memb_t = memb.T
@@ -307,13 +351,17 @@
     volt = potential
     recov = gating
     phi = ecs_start
+    shift = jnp.zeros((slots, 2), jnp.float32)
+    sent = gather(volt, cols, slots, rows_at_once)
+    got = exchange(sent.reshape(devices, capacity, LANES)).reshape(slots, LANES)
     for step in range(STEPS):
-        sent = gather(volt, cols, slots, rows_at_once)
-        got = exchange(sent.reshape(devices, capacity, LANES)).reshape(slots, LANES)
         base = steklov(ident, volt, recov, templates)
-        current, deposit = scatter(
-            got, sent, cols, conduct_cols, cell_rows, base, memb, memb_t, points // LANES, rows_at_once
+        early, deposit = scatter(
+            got, sent, shift, cols, conduct_cols, cell_rows, base, volt, memb, memb_t, points // LANES, rows_at_once
         )
+        if step + 1 < STEPS:
+            sent = gather(early, cols, slots, rows_at_once)
+            got = exchange(sent.reshape(devices, capacity, LANES)).reshape(slots, LANES)
         deposit = deposit.reshape(ecs_start.shape)
         depth = SWEEPS
         framed_phi, framed_dep = (
@@ -335,7 +383,13 @@
             inside = inside_x[:, None, None] & inside_y[None, :, None]
             current_phi = jnp.where(inside, updated, 0.0)
         phi = current_phi
-        volt, recov = update(volt, recov, current, phi.reshape(points // LANES, LANES), memb)
+        volt, recov, phi_t = update(volt, recov, early, phi.reshape(points // LANES, LANES), memb)
+        if step + 1 < STEPS:
+            own = slot_phi(phi_t, cell_rows, spot_rows, per_cell).reshape(2, devices, capacity)
+            other = exchange(jnp.concatenate([own[0], own[1]], axis=1))
+            by_source = (other[:, :capacity] - own[1]).reshape(slots)
+            by_target = (other[:, capacity:] - own[0]).reshape(slots)
+            shift = 0.05 * jnp.stack([by_source, by_target], axis=1)
     return (volt, phi)
 
 

time: 197 us -> 203 us (1.030)
  Pallas kernels: 54.4 us -> 68.6 us
  local copies, waits for them, and re-layouts: 34.5 us -> 25 us
  waiting for transfers between devices: 29.2 us -> 21.6 us
  starting transfers between devices: 55.3 us -> 60.6 us
  other arithmetic: 17.4 us -> 21.3 us
    pallas_call x2, Pallas kernels: 11.8 us -> 23.6 us  [steklov(): pl.pallas_call(steklov_kernel, grid=(count,), in_specs=[whole_block((cell...]
    unnamed x60 -> x48, local copies, waits for them, and re-layouts: 22.2 us -> 13.5 us
    all_to_all x3 -> x4, waiting for transfers between devices: 17.1 us -> 9.77 us  [exchange(): lax.all_to_all(x, ('tx', 'ty'), split_axis=0, concat_axis=0, tiled=True)]
    all_to_all x3 -> x4, starting transfers between devices: 15.9 us -> 21.7 us  [exchange(): lax.all_to_all(x, ('tx', 'ty'), split_axis=0, concat_axis=0, tiled=True)]
    mul x0 -> x1, other arithmetic: none -> 2.29 us  [on_device(): shift = 0.05 * jnp.stack([by_source, by_target], axis=1)]
    pallas_call x2 -> x3, Pallas kernels: 7.97 us -> 9.27 us  [the longest x2 8.41 us: update(): pl.pallas_call(update_kernel, out_shape=[jax.ShapeDtypeStruct(shape, jnp....]
  transfers between devices with their start and end apart: 19 -> 20, of which waited for: 6 -> 6; matrix products, arithmetic and copies ran while one was open for 9% -> 10% of each run, Pallas kernels for 15% -> 30%
where the time goes in v1:
time: 203 us; the launch traced here: 201 us
  Pallas kernels  68.6 us (34%)
  starting transfers between devices  60.6 us (30%)
  local copies, waits for them, and re-layouts  25 us (12%)
  waiting for transfers between devices  21.6 us (11%)
  other arithmetic  21.3 us (10%)
  matrix products  2.76 us (1%)
    ppermute x8, starting transfers between devices, extended(): before = lax.ppermute(last, axis, up)  25.1 us
    pallas_call x2, Pallas kernels, steklov(): pl.pallas_call(steklov_kernel, grid=(count,), in_specs=[whole_block((cell...  23.6 us
    pallas_call x2, Pallas kernels, scatter(): pl.pallas_call(scatter_kernel, grid=(slots // tile,), in_specs=[pl.BlockS...  22.3 us
    all_to_all x4, starting transfers between devices, exchange(): lax.all_to_all(x, ('tx', 'ty'), split_axis=0, concat_axis=0, tiled=True)  21.7 us
    ppermute x8, starting transfers between devices, extended(): after = lax.ppermute(leading, axis, down)  13.7 us
    unnamed x48, local copies, waits for them, and re-layouts  13.5 us
    pallas_call x2, Pallas kernels, gather(): pl.pallas_call(gather_kernel, grid=(slots // tile,), in_specs=[whole_bloc...  13.4 us
    ppermute x8, waiting for transfers between devices, extended(): after = lax.ppermute(leading, axis, down)  11.8 us
  transfers between devices with their start and end apart: 20, of which 6 were waited for; matrix products, arithmetic and copies ran while one was open for 10% of the time, Pallas kernels for 30%

profile of v1, /device:TPU:3, one launch (start us, length us, event | category | flops | bytes accessed | tf_op | source)
XLA Modules:
  0.0 201.1 jit_solution(6131506826554066644)
XLA Ops:
  8.5 6.4 %all-to-all-start = ((f32[32,1,128]{2,1,0:T(1,128)}), f32[32,1,128]{2,1,0:T(1,128)S(1)}, u32[]{:S(2)}, u32[]{:S(2)}) async-start(f32[32,1,128]{2,1,0:T(1,128)} %bitcast.2), calls=%async_computation | async-start | bytes 32768 | tf_op jit(solution)/shard_map/all_to_all | solution.py:307
  15.8 3.3 %collective-permute-start.4 = (f32[4,32,32]{2,1,0:T(8,128)S(1)}, f32[4,32,32]{2,1,0:T(8,128)S(1)}, u32[]{:S(2)}, u32[]{:S(2)}) collective-permute-start(f32[4,32,32]{2,1,0:T(8,128)S(1)} %get-tuple-element.37), channel_id=1, source_target_pairs={{0,4},{4,8},{8,12},{12,16},{16,20},{20,24},{24,28},{1,5},{5,9},{9,... | collective-permute-start | bytes 49160 | tf_op jit(solution)/shard_map/ppermute | solution.py:24
  19.2 1.9 collective-permute-start.5
  23.6 6.7 %shard_map.113.sent_ref = f32[2048,128]{1,0:T(8,128)} custom-call(f32[256,768]{1,0:T(8,128)S(1)} %copy-done, s32[2048,4]{1,0:T(8,128)S(1)} %copy.56.cols_ref), custom_call_target="tpu_custom_call" | custom-call | tf_op jit(solution)/shard_map/pallas_call | solution.py:208
  30.3 6.2 %all-to-all-start.1 = ((f32[32,64,128]{2,1,0:T(8,128)}), f32[32,64,128]{2,1,0:T(8,128)}, u32[]{:S(2)}, u32[]{:S(2)}) async-start(f32[32,64,128]{2,1,0:T(8,128)} %bitcast.4), calls=%async_computation.1 | async-start | bytes 2097152 | tf_op jit(solution)/shard_map/all_to_all | solution.py:307
  37.3 11.8 %shard_map.114.base_ref = f32[256,768]{1,0:T(8,128)} custom-call(s32[256,1]{1,0:T(8,128)} %copy.57.ident_ref, f32[256,768]{1,0:T(8,128)} %volt_ref.7, f32[256,768]{1,0:T(8,128)} %recov_ref.3, bf16[10,768,768]{2,1,0:T(8,128)(2,1)} %template_ref.3), custom_call_target="tpu_custom_call" | custom-call | flops 3019898880 | bytes 11796480 | tf_op jit(solution)/shard_map/pallas_call | solution.py:222
  51.2 3.1 %collective-permute-start.6 = (f32[40,4,32]{2,1,0:T(4,128)S(1)}, f32[40,4,32]{2,1,0:T(4,128)S(1)}, u32[]{:S(2)}, u32[]{:S(2)}) collective-permute-start(f32[40,4,32]{2,1,0:T(4,128)S(1)} %get-tuple-element.32), channel_id=1, source_target_pairs={{0,1},{1,2},{2,3},{4,5},{5,6},{6,7},{8,9},{9,10},{10,11},{12,13},{... | collective-permute-start | bytes 61448 | tf_op jit(solution)/shard_map/ppermute | solution.py:24
  57.1 5.7 %all-to-all-done.1 = f32[32,64,128]{2,1,0:T(8,128)} async-done(((f32[32,64,128]{2,1,0:T(8,128)}), f32[32,64,128]{2,1,0:T(8,128)}, u32[]{:S(2)}, u32[]{:S(2)}) %all-to-all-start.1) | async-done | bytes 1048608 | tf_op jit(solution)/shard_map/all_to_all | solution.py:307
  64.0 11.2 %shard_map.115 = (f32[256,768]{1,0:T(8,128)S(1)}, f32[256,128]{1,0:T(8,128)S(1)}) custom-call(f32[2048,128]{1,0:T(8,128)} %bitcast.5.got_ref, f32[2048,128]{1,0:T(8,128)} %shard_map.113.sent_ref, f32[2048,2]{1,0:T(8,128)S(1)} %broadcast_in_dim.99.shift_ref, s32[2048,4]{1,0:T(8,128)S(1)} %copy.56.cols_ref, f32[2048,2]{1,0:T(8,128)S(1)} %copy.60.conduct_ref, ...), custom_call_target="tpu_custom_call" | custom-call | tf_op jit(solution)/shard_map/pallas_call | solution.py:243
  76.8 1.9 collective-permute-start
  80.5 2.4 %collective-permute-start.1 = (f32[4,32,32]{2,1,0:T(8,128)S(1)}, f32[4,32,32]{2,1,0:T(8,128)S(1)}, u32[]{:S(2)}, u32[]{:S(2)}) collective-permute-start(f32[4,32,32]{2,1,0:T(8,128)S(1)} %slice.313), channel_id=1, source_target_pairs={{4,0},{8,4},{12,8},{16,12},{20,16},{24,20},{28,24},{5,1},{9,5},{13... | collective-permute-start | bytes 49160 | tf_op jit(solution)/shard_map/ppermute | solution.py:25
  84.9 2.1 %collective-permute-done.1 = f32[4,32,32]{2,1,0:T(8,128)S(1)} collective-permute-done((f32[4,32,32]{2,1,0:T(8,128)S(1)}, f32[4,32,32]{2,1,0:T(8,128)S(1)}, u32[]{:S(2)}, u32[]{:S(2)}) %collective-permute-start.1) | collective-permute-done | bytes 16416 | tf_op jit(solution)/shard_map/ppermute | solution.py:25
  87.0 3.7 %collective-permute-start.2 = (f32[40,4,32]{2,1,0:T(4,128)S(1)}, f32[40,4,32]{2,1,0:T(4,128)S(1)}, u32[]{:S(2)}, u32[]{:S(2)}) collective-permute-start(f32[40,4,32]{2,1,0:T(4,128)S(1)} %get-tuple-element.30), channel_id=1, source_target_pairs={{0,1},{1,2},{2,3},{4,5},{5,6},{6,7},{8,9},{9,10},{10,11},{12,13},{... | collective-permute-start | bytes 61448 | tf_op jit(solution)/shard_map/ppermute | solution.py:24
  90.7 1.5 collective-permute-start.3
  93.4 2.5 %collective-permute-done.3 = f32[40,4,32]{2,1,0:T(4,128)S(1)} collective-permute-done((f32[40,4,32]{2,1,0:T(4,128)S(1)}, f32[40,4,32]{2,1,0:T(4,128)S(1)}, u32[]{:S(2)}, u32[]{:S(2)}) %collective-permute-start.3) | collective-permute-done | bytes 20512 | tf_op jit(solution)/shard_map/ppermute | solution.py:25
  102.8 3.6 %shard_map.116 = (f32[256,768]{1,0:T(8,128)S(1)}, f32[256,768]{1,0:T(8,128)S(1)}, f32[128,256]{1,0:T(8,128)S(1)}) custom-call(f32[256,768]{1,0:T(8,128)S(1)} %copy-done.1, f32[256,768]{1,0:T(8,128)S(1)} %copy-done.5, f32[256,768]{1,0:T(8,128)S(1)} %copy-done.9, f32[256,128]{1,0:T(8,128)S(1)} %reshape.492.phi_ref, s32[256,12]{1,0:T(8,128)S(1)} %reshape.490.memb_ref), custom_call_target="tpu_custom_call" | custom-call | tf_op jit(solution)/shard_map/pallas_call | solution.py:270
  109.9 3.2 %all-to-all-start.3 = ((f32[32,1,128]{2,1,0:T(1,128)}), f32[32,1,128]{2,1,0:T(1,128)S(1)}, u32[]{:S(2)}, u32[]{:S(2)}) async-start(f32[32,1,128]{2,1,0:T(1,128)} %bitcast.14), calls=%async_computation.3 | async-start | bytes 32768 | tf_op jit(solution)/shard_map/all_to_all | solution.py:307
  114.3 6.7 %shard_map.117.sent_ref = f32[2048,128]{1,0:T(8,128)} custom-call(f32[256,768]{1,0:T(8,128)S(1)} %copy-done.10, s32[2048,4]{1,0:T(8,128)S(1)} %copy.56.cols_ref), custom_call_target="tpu_custom_call" | custom-call | tf_op jit(solution)/shard_map/pallas_call | solution.py:208
  121.0 5.9 %all-to-all-start.2 = ((f32[32,64,128]{2,1,0:T(8,128)}), f32[32,64,128]{2,1,0:T(8,128)}, u32[]{:S(2)}, u32[]{:S(2)}) async-start(f32[32,64,128]{2,1,0:T(8,128)} %bitcast.12), calls=%async_computation.2 | async-start | bytes 2097152 | tf_op jit(solution)/shard_map/all_to_all | solution.py:307
  127.8 3.3 %collective-permute-start.12 = (f32[4,32,32]{2,1,0:T(8,128)S(1)}, f32[4,32,32]{2,1,0:T(8,128)S(1)}, u32[]{:S(2)}, u32[]{:S(2)}) collective-permute-start(f32[4,32,32]{2,1,0:T(8,128)S(1)} %get-tuple-element.34), channel_id=1, source_target_pairs={{0,4},{4,8},{8,12},{12,16},{16,20},{20,24},{24,28},{1,5},{5,9},{9,... | collective-permute-start | bytes 49160 | tf_op jit(solution)/shard_map/ppermute | solution.py:24
  131.1 2.1 %collective-permute-start.13 = (f32[4,32,32]{2,1,0:T(8,128)S(1)}, f32[4,32,32]{2,1,0:T(8,128)S(1)}, u32[]{:S(2)}, u32[]{:S(2)}) collective-permute-start(f32[4,32,32]{2,1,0:T(8,128)S(1)} %get-tuple-element.35), channel_id=1, source_target_pairs={{4,0},{8,4},{12,8},{16,12},{20,16},{24,20},{28,24},{5,1},{9,5},{13... | collective-permute-start | bytes 49160 | tf_op jit(solution)/shard_map/ppermute | solution.py:25
  133.3 11.9 %shard_map.119.base_ref = f32[256,768]{1,0:T(8,128)} custom-call(s32[256,1]{1,0:T(8,128)} %copy.57.ident_ref, f32[256,768]{1,0:T(8,128)} %copy-done.2, f32[256,768]{1,0:T(8,128)} %copy-done.6, bf16[10,768,768]{2,1,0:T(8,128)(2,1)} %template_ref.3), custom_call_target="tpu_custom_call" | custom-call | flops 3019898880 | bytes 11796480 | tf_op jit(solution)/shard_map/pallas_call | solution.py:222
  146.8 2.3 %broadcast_multiply_fusion.shift_ref = f32[2048,2]{1,0:T(8,128)} fusion(f32[2048,2]{1,0:T(8,128)} %copy.62), kind=kLoop, calls=%fused_computation.80 | loop fusion | flops 4096 | bytes 32768 | tf_op jit(solution)/shard_map/mul | solution.py:392
  149.0 4.1 %all-to-all-done.2 = f32[32,64,128]{2,1,0:T(8,128)} async-done(((f32[32,64,128]{2,1,0:T(8,128)}), f32[32,64,128]{2,1,0:T(8,128)}, u32[]{:S(2)}, u32[]{:S(2)}) %all-to-all-start.2) | async-done | bytes 1048608 | tf_op jit(solution)/shard_map/all_to_all | solution.py:307
  155.5 11.2 %shard_map.120 = (f32[256,768]{1,0:T(8,128)S(1)}, f32[256,128]{1,0:T(8,128)S(1)}) custom-call(f32[2048,128]{1,0:T(8,128)} %bitcast.13.got_ref, f32[2048,128]{1,0:T(8,128)} %shard_map.117.sent_ref, f32[2048,2]{1,0:T(8,128)S(1)} %copy-done.4, s32[2048,4]{1,0:T(8,128)S(1)} %copy.56.cols_ref, f32[2048,2]{1,0:T(8,128)S(1)} %copy.60.conduct_ref, ...), custom_call_target="tpu_custom_call" | custom-call | tf_op jit(solution)/shard_map/pallas_call | solution.py:243
  167.6 1.9 collective-permute-start.8
  170.6 3.8 %collective-permute-start.14 = (f32[40,4,32]{2,1,0:T(4,128)S(1)}, f32[40,4,32]{2,1,0:T(4,128)S(1)}, u32[]{:S(2)}, u32[]{:S(2)}) collective-permute-start(f32[40,4,32]{2,1,0:T(4,128)S(1)} %get-tuple-element.28), channel_id=1, source_target_pairs={{0,1},{1,2},{2,3},{4,5},{5,6},{6,7},{8,9},{9,10},{10,11},{12,13},{... | collective-permute-start | bytes 61448 | tf_op jit(solution)/shard_map/ppermute | solution.py:24
  175.9 1.9 collective-permute-start.9
  177.9 4.5 %collective-permute-done.9 = f32[4,32,32]{2,1,0:T(8,128)S(1)} collective-permute-done((f32[4,32,32]{2,1,0:T(8,128)S(1)}, f32[4,32,32]{2,1,0:T(8,128)S(1)}, u32[]{:S(2)}, u32[]{:S(2)}) %collective-permute-start.9) | collective-permute-done | bytes 16416 | tf_op jit(solution)/shard_map/ppermute | solution.py:25
  182.4 4.0 %collective-permute-start.10 = (f32[40,4,32]{2,1,0:T(4,128)S(1)}, f32[40,4,32]{2,1,0:T(4,128)S(1)}, u32[]{:S(2)}, u32[]{:S(2)}) collective-permute-start(f32[40,4,32]{2,1,0:T(4,128)S(1)} %get-tuple-element.26), channel_id=1, source_target_pairs={{0,1},{1,2},{2,3},{4,5},{5,6},{6,7},{8,9},{9,10},{10,11},{12,13},{... | collective-permute-start | bytes 61448 | tf_op jit(solution)/shard_map/ppermute | solution.py:24
  188.9 2.7 %collective-permute-done.11 = f32[40,4,32]{2,1,0:T(4,128)S(1)} collective-permute-done((f32[40,4,32]{2,1,0:T(4,128)S(1)}, f32[40,4,32]{2,1,0:T(4,128)S(1)}, u32[]{:S(2)}, u32[]{:S(2)}) %collective-permute-start.11) | collective-permute-done | bytes 20512 | tf_op jit(solution)/shard_map/ppermute | solution.py:25
  196.3 4.8 %shard_map.121 = (f32[256,768]{1,0:T(8,128)}, f32[256,768]{1,0:T(8,128)}, f32[128,256]{1,0:T(8,128)}) custom-call(f32[256,768]{1,0:T(8,128)S(1)} %copy-done.3, f32[256,768]{1,0:T(8,128)S(1)} %copy-done.7, f32[256,768]{1,0:T(8,128)S(1)} %copy-done.14, f32[256,128]{1,0:T(8,128)S(1)} %reshape.496.phi_ref, s32[256,12]{1,0:T(8,128)S(1)} %reshape.490.memb_ref), custom_call_target="tpu_custom_call" | custom-call | tf_op jit(solution)/shard_map/pallas_call | solution.py:270
  (160 shorter events, 51.5 us)
Async XLA Ops:
  0.6 22.9 %copy-start = (f32[256,768]{1,0:T(8,128)S(1)}, f32[256,768]{1,0:T(8,128)}, u32[]{:S(2)}) copy-start(f32[256,768]{1,0:T(8,128)} %volt_ref.7) | copy-start | bytes 2359300
  6.4 30.1 %copy-start.20 = (s32[256]{0:T(256)S(1)}, s32[256]{0:T(256)}, u32[]{:S(2)}) copy-start(s32[256]{0:T(256)} %param.14) | copy-start | bytes 3076
  8.5 14.2 %all-to-all-start = ((f32[32,1,128]{2,1,0:T(1,128)}), f32[32,1,128]{2,1,0:T(1,128)S(1)}, u32[]{:S(2)}, u32[]{:S(2)}) async-start(f32[32,1,128]{2,1,0:T(1,128)} %bitcast.2), calls=%async_computation | async-start | bytes 32768 | tf_op jit(solution)/shard_map/all_to_all | solution.py:307
  15.8 34.2 %collective-permute-start.4 = (f32[4,32,32]{2,1,0:T(8,128)S(1)}, f32[4,32,32]{2,1,0:T(8,128)S(1)}, u32[]{:S(2)}, u32[]{:S(2)}) collective-permute-start(f32[4,32,32]{2,1,0:T(8,128)S(1)} %get-tuple-element.37), channel_id=1, source_target_pairs={{0,4},{4,8},{8,12},{12,16},{16,20},{20,24},{24,28},{1,5},{5,9},{9,... | collective-permute-start | bytes 49160 | tf_op jit(solution)/shard_map/ppermute | solution.py:24
  19.2 31.9 %collective-permute-start.5 = (f32[4,32,32]{2,1,0:T(8,128)S(1)}, f32[4,32,32]{2,1,0:T(8,128)S(1)}, u32[]{:S(2)}, u32[]{:S(2)}) collective-permute-start(f32[4,32,32]{2,1,0:T(8,128)S(1)} %get-tuple-element.36), channel_id=1, source_target_pairs={{4,0},{8,4},{12,8},{16,12},{20,16},{24,20},{28,24},{5,1},{9,5},{13... | collective-permute-start | bytes 49160 | tf_op jit(solution)/shard_map/ppermute | solution.py:25
  30.3 32.5 %all-to-all-start.1 = ((f32[32,64,128]{2,1,0:T(8,128)}), f32[32,64,128]{2,1,0:T(8,128)}, u32[]{:S(2)}, u32[]{:S(2)}) async-start(f32[32,64,128]{2,1,0:T(8,128)} %bitcast.4), calls=%async_computation.1 | async-start | bytes 2097152 | tf_op jit(solution)/shard_map/all_to_all | solution.py:307
  37.3 12.4 %copy-start.19 = (s32[3072]{0:T(1024)S(1)}, s32[3072]{0:T(1024)}, u32[]{:S(2)}) copy-start(s32[3072]{0:T(1024)} %param.19) | copy-start | bytes 36868
  49.1 13.8 %copy-start.1 = (f32[256,768]{1,0:T(8,128)S(1)}, f32[256,768]{1,0:T(8,128)}, u32[]{:S(2)}) copy-start(f32[256,768]{1,0:T(8,128)} %volt_ref.7) | copy-start | bytes 2359300
  51.1 4.9 %copy-start.16 = (f32[40,32,32]{2,1,0:T(8,128)}, f32[40,32,32]{2,1,0:T(8,128)S(1)}, u32[]{:S(2)}) copy-start(f32[40,32,32]{2,1,0:T(8,128)S(1)} %constant_dynamic-update-slice_fusion.3) | copy-start | bytes 491524
  51.2 41.0 %collective-permute-start.6 = (f32[40,4,32]{2,1,0:T(4,128)S(1)}, f32[40,4,32]{2,1,0:T(4,128)S(1)}, u32[]{:S(2)}, u32[]{:S(2)}) collective-permute-start(f32[40,4,32]{2,1,0:T(4,128)S(1)} %get-tuple-element.32), channel_id=1, source_target_pairs={{0,1},{1,2},{2,3},{4,5},{5,6},{6,7},{8,9},{9,10},{10,11},{12,13},{... | collective-permute-start | bytes 61448 | tf_op jit(solution)/shard_map/ppermute | solution.py:24
  54.3 38.0 %collective-permute-start.7 = (f32[40,4,32]{2,1,0:T(4,128)S(1)}, f32[40,4,32]{2,1,0:T(4,128)S(1)}, u32[]{:S(2)}, u32[]{:S(2)}) collective-permute-start(f32[40,4,32]{2,1,0:T(4,128)S(1)} %get-tuple-element.33), channel_id=1, source_target_pairs={{1,0},{2,1},{3,2},{5,4},{6,5},{7,6},{9,8},{10,9},{11,10},{13,12},{... | collective-permute-start | bytes 61448 | tf_op jit(solution)/shard_map/ppermute | solution.py:25
  76.8 6.1 %collective-permute-start = (f32[4,32,32]{2,1,0:T(8,128)}, f32[4,32,32]{2,1,0:T(8,128)}, u32[]{:S(2)}, u32[]{:S(2)}) collective-permute-start(f32[4,32,32]{2,1,0:T(8,128)} %slice.311), channel_id=1, source_target_pairs={{0,4},{4,8},{8,12},{12,16},{16,20},{20,24},{24,28},{1,5},{5,9},{9,... | collective-permute-start | bytes 49160 | tf_op jit(solution)/shard_map/ppermute | solution.py:24
  80.5 6.5 %collective-permute-start.1 = (f32[4,32,32]{2,1,0:T(8,128)S(1)}, f32[4,32,32]{2,1,0:T(8,128)S(1)}, u32[]{:S(2)}, u32[]{:S(2)}) collective-permute-start(f32[4,32,32]{2,1,0:T(8,128)S(1)} %slice.313), channel_id=1, source_target_pairs={{4,0},{8,4},{12,8},{16,12},{20,16},{24,20},{28,24},{5,1},{9,5},{13... | collective-permute-start | bytes 49160 | tf_op jit(solution)/shard_map/ppermute | solution.py:25
  87.0 6.4 %collective-permute-start.2 = (f32[40,4,32]{2,1,0:T(4,128)S(1)}, f32[40,4,32]{2,1,0:T(4,128)S(1)}, u32[]{:S(2)}, u32[]{:S(2)}) collective-permute-start(f32[40,4,32]{2,1,0:T(4,128)S(1)} %get-tuple-element.30), channel_id=1, source_target_pairs={{0,1},{1,2},{2,3},{4,5},{5,6},{6,7},{8,9},{9,10},{10,11},{12,13},{... | collective-permute-start | bytes 61448 | tf_op jit(solution)/shard_map/ppermute | solution.py:24
  90.7 5.2 %collective-permute-start.3 = (f32[40,4,32]{2,1,0:T(4,128)S(1)}, f32[40,4,32]{2,1,0:T(4,128)S(1)}, u32[]{:S(2)}, u32[]{:S(2)}) collective-permute-start(f32[40,4,32]{2,1,0:T(4,128)S(1)} %get-tuple-element.31), channel_id=1, source_target_pairs={{1,0},{2,1},{3,2},{5,4},{6,5},{7,6},{9,8},{10,9},{11,10},{13,12},{... | collective-permute-start | bytes 61448 | tf_op jit(solution)/shard_map/ppermute | solution.py:25
  96.0 1.4 copy-start.17
  96.7 1.3 copy-start.15
  96.7 1.3 copy-start.18
  109.9 11.0 %all-to-all-start.3 = ((f32[32,1,128]{2,1,0:T(1,128)}), f32[32,1,128]{2,1,0:T(1,128)S(1)}, u32[]{:S(2)}, u32[]{:S(2)}) async-start(f32[32,1,128]{2,1,0:T(1,128)} %bitcast.14), calls=%async_computation.3 | async-start | bytes 32768 | tf_op jit(solution)/shard_map/all_to_all | solution.py:307
  121.0 32.1 %all-to-all-start.2 = ((f32[32,64,128]{2,1,0:T(8,128)}), f32[32,64,128]{2,1,0:T(8,128)}, u32[]{:S(2)}, u32[]{:S(2)}) async-start(f32[32,64,128]{2,1,0:T(8,128)} %bitcast.12), calls=%async_computation.2 | async-start | bytes 2097152 | tf_op jit(solution)/shard_map/all_to_all | solution.py:307
  127.8 41.8 %collective-permute-start.12 = (f32[4,32,32]{2,1,0:T(8,128)S(1)}, f32[4,32,32]{2,1,0:T(8,128)S(1)}, u32[]{:S(2)}, u32[]{:S(2)}) collective-permute-start(f32[4,32,32]{2,1,0:T(8,128)S(1)} %get-tuple-element.34), channel_id=1, source_target_pairs={{0,4},{4,8},{8,12},{12,16},{16,20},{20,24},{24,28},{1,5},{5,9},{9,... | collective-permute-start | bytes 49160 | tf_op jit(solution)/shard_map/ppermute | solution.py:24
  131.1 38.4 %collective-permute-start.13 = (f32[4,32,32]{2,1,0:T(8,128)S(1)}, f32[4,32,32]{2,1,0:T(8,128)S(1)}, u32[]{:S(2)}, u32[]{:S(2)}) collective-permute-start(f32[4,32,32]{2,1,0:T(8,128)S(1)} %get-tuple-element.35), channel_id=1, source_target_pairs={{4,0},{8,4},{12,8},{16,12},{20,16},{24,20},{28,24},{5,1},{9,5},{13... | collective-permute-start | bytes 49160 | tf_op jit(solution)/shard_map/ppermute | solution.py:25
  133.3 19.8 %copy-start.3 = (f32[256,768]{1,0:T(8,128)S(1)}, f32[256,768]{1,0:T(8,128)}, u32[]{:S(2)}) copy-start(f32[256,768]{1,0:T(8,128)} %copy-done.2) | copy-start | bytes 2359300
  153.1 1.2 copy-start.4
  167.6 10.2 %collective-permute-start.8 = (f32[4,32,32]{2,1,0:T(8,128)S(1)}, f32[4,32,32]{2,1,0:T(8,128)S(1)}, u32[]{:S(2)}, u32[]{:S(2)}) collective-permute-start(f32[4,32,32]{2,1,0:T(8,128)S(1)} %slice.352), channel_id=1, source_target_pairs={{0,4},{4,8},{8,12},{12,16},{16,20},{20,24},{24,28},{1,5},{5,9},{9,... | collective-permute-start | bytes 49160 | tf_op jit(solution)/shard_map/ppermute | solution.py:24
  170.6 17.2 %collective-permute-start.14 = (f32[40,4,32]{2,1,0:T(4,128)S(1)}, f32[40,4,32]{2,1,0:T(4,128)S(1)}, u32[]{:S(2)}, u32[]{:S(2)}) collective-permute-start(f32[40,4,32]{2,1,0:T(4,128)S(1)} %get-tuple-element.28), channel_id=1, source_target_pairs={{0,1},{1,2},{2,3},{4,5},{5,6},{6,7},{8,9},{9,10},{10,11},{12,13},{... | collective-permute-start | bytes 61448 | tf_op jit(solution)/shard_map/ppermute | solution.py:24
  174.4 13.4 %collective-permute-start.15 = (f32[40,4,32]{2,1,0:T(4,128)S(1)}, f32[40,4,32]{2,1,0:T(4,128)S(1)}, u32[]{:S(2)}, u32[]{:S(2)}) collective-permute-start(f32[40,4,32]{2,1,0:T(4,128)S(1)} %get-tuple-element.29), channel_id=1, source_target_pairs={{1,0},{2,1},{3,2},{5,4},{6,5},{7,6},{9,8},{10,9},{11,10},{13,12},{... | collective-permute-start | bytes 61448 | tf_op jit(solution)/shard_map/ppermute | solution.py:25
  175.9 6.5 %collective-permute-start.9 = (f32[4,32,32]{2,1,0:T(8,128)S(1)}, f32[4,32,32]{2,1,0:T(8,128)S(1)}, u32[]{:S(2)}, u32[]{:S(2)}) collective-permute-start(f32[4,32,32]{2,1,0:T(8,128)S(1)} %slice.354), channel_id=1, source_target_pairs={{4,0},{8,4},{12,8},{16,12},{20,16},{24,20},{28,24},{5,1},{9,5},{13... | collective-permute-start | bytes 49160 | tf_op jit(solution)/shard_map/ppermute | solution.py:25
  182.4 6.5 %collective-permute-start.10 = (f32[40,4,32]{2,1,0:T(4,128)S(1)}, f32[40,4,32]{2,1,0:T(4,128)S(1)}, u32[]{:S(2)}, u32[]{:S(2)}) collective-permute-start(f32[40,4,32]{2,1,0:T(4,128)S(1)} %get-tuple-element.26), channel_id=1, source_target_pairs={{0,1},{1,2},{2,3},{4,5},{5,6},{6,7},{8,9},{9,10},{10,11},{12,13},{... | collective-permute-start | bytes 61448 | tf_op jit(solution)/shard_map/ppermute | solution.py:24
  186.4 5.2 %collective-permute-start.11 = (f32[40,4,32]{2,1,0:T(4,128)S(1)}, f32[40,4,32]{2,1,0:T(4,128)S(1)}, u32[]{:S(2)}, u32[]{:S(2)}) collective-permute-start(f32[40,4,32]{2,1,0:T(4,128)S(1)} %get-tuple-element.27), channel_id=1, source_target_pairs={{1,0},{2,1},{3,2},{5,4},{6,5},{7,6},{9,8},{10,9},{11,10},{13,12},{... | collective-permute-start | bytes 61448 | tf_op jit(solution)/shard_map/ppermute | solution.py:25
  193.1 3.1 %copy-start.7 = (f32[256,768]{1,0:T(8,128)S(1)}, f32[256,768]{1,0:T(8,128)}, u32[]{:S(2)}) copy-start(f32[256,768]{1,0:T(8,128)} %copy-done.6) | copy-start | bytes 2359300
  193.1 3.1 %copy-start.14 = (f32[256,768]{1,0:T(8,128)S(1)}, f32[256,768]{1,0:T(8,128)}, u32[]{:S(2)}) copy-start(f32[256,768]{1,0:T(8,128)} %copy-done.13) | copy-start | bytes 2359300
  (9 other events, 9.2 us)

commit v2 on v1

--- a/solution.py
+++ b/solution.py
@@ -230,7 +230,7 @@
         ],
         out_specs=whole_block((cells, nodes)),
         out_shape=jax.ShapeDtypeStruct((cells, nodes), jnp.float32),
-        compiler_params=pltpu.CompilerParams(vmem_limit_bytes=56 * 1024 * 1024),
+        compiler_params=params(),
         cost_estimate=pl.CostEstimate(
             flops=2 * count * cells * nodes * nodes, bytes_accessed=2 * count * nodes * nodes, transcendentals=0
         ),
@@ -361,6 +361,7 @@
         )
         if step + 1 < STEPS:
             sent = gather(early, cols, slots, rows_at_once)
+            deposit, sent = lax.optimization_barrier((deposit, sent))
             got = exchange(sent.reshape(devices, capacity, LANES)).reshape(slots, LANES)
         deposit = deposit.reshape(ecs_start.shape)
         depth = SWEEPS
@@ -386,6 +387,7 @@
         volt, recov, phi_t = update(volt, recov, early, phi.reshape(points // LANES, LANES), memb)
         if step + 1 < STEPS:
             own = slot_phi(phi_t, cell_rows, spot_rows, per_cell).reshape(2, devices, capacity)
+            own, got = lax.optimization_barrier((own, got))
             other = exchange(jnp.concatenate([own[0], own[1]], axis=1))
             by_source = (other[:, :capacity] - own[1]).reshape(slots)
             by_target = (other[:, capacity:] - own[0]).reshape(slots)

time: 203 us -> 214 us (1.054)
  local copies, waits for them, and re-layouts: 25 us -> 38 us
  Pallas kernels: 68.6 us -> 56 us
  starting transfers between devices: 60.6 us -> 69.5 us
    unnamed x48 -> x74, local copies, waits for them, and re-layouts: 13.5 us -> 25.9 us
    pallas_call x2, Pallas kernels: 23.6 us -> 11.8 us  [steklov(): pl.pallas_call(steklov_kernel, grid=(count,), in_specs=[whole_block((cell...]
    ppermute x8, waiting for transfers between devices: 0.02 us -> 11 us  [extended(): before = lax.ppermute(last, axis, up)]
    all_to_all x4, starting transfers between devices: 21.7 us -> 30.1 us  [exchange(): lax.all_to_all(x, ('tx', 'ty'), split_axis=0, concat_axis=0, tiled=True)]
    all_to_all x4, waiting for transfers between devices: 9.77 us -> 2.98 us  [exchange(): lax.all_to_all(x, ('tx', 'ty'), split_axis=0, concat_axis=0, tiled=True)]
    ppermute x8, waiting for transfers between devices: 11.8 us -> 6.96 us  [extended(): after = lax.ppermute(leading, axis, down)]
  transfers between devices with their start and end apart: 20 -> 20, of which waited for: 6 -> 4; matrix products, arithmetic and copies ran while one was open for 10% -> 14% of each run, Pallas kernels for 30% -> 24%
where the time goes in v2:
time: 214 us; the launch traced here: 212 us
  starting transfers between devices  69.5 us (32%)
  Pallas kernels  56 us (26%)
  local copies, waits for them, and re-layouts  38 us (18%)
  other arithmetic  23.2 us (11%)
  waiting for transfers between devices  21 us (10%)
  matrix products  2.76 us (1%)
    all_to_all x4, starting transfers between devices, exchange(): lax.all_to_all(x, ('tx', 'ty'), split_axis=0, concat_axis=0, tiled=True)  30.1 us
    unnamed x74, local copies, waits for them, and re-layouts  25.9 us
    ppermute x8, starting transfers between devices, extended(): before = lax.ppermute(last, axis, up)  25.7 us
    pallas_call x2, Pallas kernels, scatter(): pl.pallas_call(scatter_kernel, grid=(slots // tile,), in_specs=[pl.BlockS...  22.2 us
    ppermute x8, starting transfers between devices, extended(): after = lax.ppermute(leading, axis, down)  13.7 us
    pallas_call x2, Pallas kernels, gather(): pl.pallas_call(gather_kernel, grid=(slots // tile,), in_specs=[whole_bloc...  12.7 us
    pallas_call x2, Pallas kernels, steklov(): pl.pallas_call(steklov_kernel, grid=(count,), in_specs=[whole_block((cell...  11.8 us
    ppermute x8, waiting for transfers between devices, extended(): before = lax.ppermute(last, axis, up)  11 us
  transfers between devices with their start and end apart: 20, of which 4 were waited for; matrix products, arithmetic and copies ran while one was open for 14% of the time, Pallas kernels for 24%

profile of v2, /device:TPU:3, one launch (start us, length us, event | category | flops | bytes accessed | tf_op | source)
XLA Modules:
  0.0 212.1 jit_solution(1223479323093888737)
XLA Ops:
  5.0 1.5 fusion
  9.1 6.4 %all-to-all-start = ((f32[32,1,128]{2,1,0:T(1,128)}), f32[32,1,128]{2,1,0:T(1,128)S(1)}, u32[]{:S(2)}, u32[]{:S(2)}) async-start(f32[32,1,128]{2,1,0:T(1,128)} %bitcast.2), calls=%async_computation | async-start | bytes 32768 | tf_op jit(solution)/shard_map/all_to_all | solution.py:307
  16.2 3.3 %collective-permute-start.4 = (f32[4,32,32]{2,1,0:T(8,128)}, f32[4,32,32]{2,1,0:T(8,128)}, u32[]{:S(2)}, u32[]{:S(2)}) collective-permute-start(f32[4,32,32]{2,1,0:T(8,128)} %get-tuple-element.43), channel_id=1, source_target_pairs={{0,4},{4,8},{8,12},{12,16},{16,20},{20,24},{24,28},{1,5},{5,9},{9,... | collective-permute-start | bytes 49160 | tf_op jit(solution)/shard_map/ppermute | solution.py:24
  19.5 1.9 collective-permute-start.5
  25.7 6.7 %shard_map.113.sent_ref = f32[2048,128]{1,0:T(8,128)} custom-call(f32[256,768]{1,0:T(8,128)S(1)} %copy-done.2, s32[2048,4]{1,0:T(8,128)S(1)} %copy.56.cols_ref), custom_call_target="tpu_custom_call" | custom-call | tf_op jit(solution)/shard_map/pallas_call | solution.py:208
  32.4 6.2 %all-to-all-start.1 = ((f32[32,64,128]{2,1,0:T(8,128)}), f32[32,64,128]{2,1,0:T(8,128)}, u32[]{:S(2)}, u32[]{:S(2)}) async-start(f32[32,64,128]{2,1,0:T(8,128)} %bitcast.4), calls=%async_computation.1 | async-start | bytes 2097152 | tf_op jit(solution)/shard_map/all_to_all | solution.py:307
  38.8 4.3 %copy-done = bf16[10,768,768]{2,1,0:T(8,128)(2,1)S(1)} copy-done((bf16[10,768,768]{2,1,0:T(8,128)(2,1)S(1)}, bf16[10,768,768]{2,1,0:T(8,128)(2,1)}, u32[]{:S(2)}) %copy-start) | copy-done | bytes 11796504
  43.2 5.9 %shard_map.114.base_ref = f32[256,768]{1,0:T(8,128)S(1)} custom-call(s32[256,1]{1,0:T(8,128)S(1)} %copy.57.ident_ref, f32[256,768]{1,0:T(8,128)S(1)} %copy-done.2, f32[256,768]{1,0:T(8,128)S(1)} %copy-done.7, bf16[10,768,768]{2,1,0:T(8,128)(2,1)S(1)} %copy-done), custom_call_target="tpu_custom_call" | custom-call | flops 3019898880 | bytes 11796480 | tf_op jit(solution)/shard_map/pallas_call | solution.py:222
  53.3 3.1 %collective-permute-start.6 = (f32[40,4,32]{2,1,0:T(4,128)}, f32[40,4,32]{2,1,0:T(4,128)S(1)}, u32[]{:S(2)}, u32[]{:S(2)}) collective-permute-start(f32[40,4,32]{2,1,0:T(4,128)} %get-tuple-element.38), channel_id=1, source_target_pairs={{0,1},{1,2},{2,3},{4,5},{5,6},{6,7},{8,9},{9,10},{10,11},{12,13},{... | collective-permute-start | bytes 61448 | tf_op jit(solution)/shard_map/ppermute | solution.py:24
  62.0 3.0 %all-to-all-done.1 = f32[32,64,128]{2,1,0:T(8,128)} async-done(((f32[32,64,128]{2,1,0:T(8,128)}), f32[32,64,128]{2,1,0:T(8,128)}, u32[]{:S(2)}, u32[]{:S(2)}) %all-to-all-start.1) | async-done | bytes 1048608 | tf_op jit(solution)/shard_map/all_to_all | solution.py:307
  66.2 11.2 %shard_map.115 = (f32[256,768]{1,0:T(8,128)S(1)}, f32[256,128]{1,0:T(8,128)S(1)}) custom-call(f32[2048,128]{1,0:T(8,128)} %bitcast.5.got_ref, f32[2048,128]{1,0:T(8,128)} %shard_map.113.sent_ref, f32[2048,2]{1,0:T(8,128)S(1)} %broadcast_in_dim.99.shift_ref, s32[2048,4]{1,0:T(8,128)S(1)} %copy.56.cols_ref, f32[2048,2]{1,0:T(8,128)S(1)} %copy.60.conduct_ref, ...), custom_call_target="tpu_custom_call" | custom-call | tf_op jit(solution)/shard_map/pallas_call | solution.py:243
  77.4 6.0 %shard_map.116.sent_ref = f32[2048,128]{1,0:T(8,128)S(1)} custom-call(f32[256,768]{1,0:T(8,128)S(1)} %get-tuple-element.14.volt_ref.early_ref, s32[2048,4]{1,0:T(8,128)S(1)} %copy.56.cols_ref), custom_call_target="tpu_custom_call" | custom-call | tf_op jit(solution)/shard_map/pallas_call | solution.py:208
  85.1 1.9 collective-permute-start
  89.5 2.6 %collective-permute-start.1 = (f32[4,32,32]{2,1,0:T(8,128)S(1)}, f32[4,32,32]{2,1,0:T(8,128)S(1)}, u32[]{:S(2)}, u32[]{:S(2)}) collective-permute-start(f32[4,32,32]{2,1,0:T(8,128)S(1)} %slice.311), channel_id=1, source_target_pairs={{4,0},{8,4},{12,8},{16,12},{20,16},{24,20},{28,24},{5,1},{9,5},{13... | collective-permute-start | bytes 49160 | tf_op jit(solution)/shard_map/ppermute | solution.py:25
  92.1 5.6 %all-to-all-start.2 = ((f32[32,64,128]{2,1,0:T(8,128)}), f32[32,64,128]{2,1,0:T(8,128)}, u32[]{:S(2)}, u32[]{:S(2)}) async-start(f32[32,64,128]{2,1,0:T(8,128)} %bitcast.40), calls=%async_computation.2 | async-start | bytes 2097152 | tf_op jit(solution)/shard_map/all_to_all | solution.py:307
  99.7 3.1 %collective-permute-start.2 = (f32[40,4,32]{2,1,0:T(4,128)S(1)}, f32[40,4,32]{2,1,0:T(4,128)S(1)}, u32[]{:S(2)}, u32[]{:S(2)}) collective-permute-start(f32[40,4,32]{2,1,0:T(4,128)S(1)} %get-tuple-element.36), channel_id=1, source_target_pairs={{0,1},{1,2},{2,3},{4,5},{5,6},{6,7},{8,9},{9,10},{10,11},{12,13},{... | collective-permute-start | bytes 61448 | tf_op jit(solution)/shard_map/ppermute | solution.py:24
  105.4 11.0 %collective-permute-done.2 = f32[40,4,32]{2,1,0:T(4,128)S(1)} collective-permute-done((f32[40,4,32]{2,1,0:T(4,128)S(1)}, f32[40,4,32]{2,1,0:T(4,128)S(1)}, u32[]{:S(2)}, u32[]{:S(2)}) %collective-permute-start.2) | collective-permute-done | bytes 20512 | tf_op jit(solution)/shard_map/ppermute | solution.py:24
  123.4 3.6 %shard_map.117 = (f32[256,768]{1,0:T(8,128)S(1)}, f32[256,768]{1,0:T(8,128)S(1)}, f32[128,256]{1,0:T(8,128)S(1)}) custom-call(f32[256,768]{1,0:T(8,128)S(1)} %copy-done.2, f32[256,768]{1,0:T(8,128)S(1)} %copy-done.8, f32[256,768]{1,0:T(8,128)S(1)} %copy-done.13, f32[256,128]{1,0:T(8,128)S(1)} %reshape.490.phi_ref, s32[256,12]{1,0:T(8,128)S(1)} %reshape.488.memb_ref), custom_call_target="tpu_custom_call" | custom-call | tf_op jit(solution)/shard_map/pallas_call | solution.py:270
  130.5 3.9 %collective-permute-start.12 = (f32[4,32,32]{2,1,0:T(8,128)S(1)}, f32[4,32,32]{2,1,0:T(8,128)S(1)}, u32[]{:S(2)}, u32[]{:S(2)}) collective-permute-start(f32[4,32,32]{2,1,0:T(8,128)S(1)} %get-tuple-element.40), channel_id=1, source_target_pairs={{0,4},{4,8},{8,12},{12,16},{16,20},{20,24},{24,28},{1,5},{5,9},{9,... | collective-permute-start | bytes 49160 | tf_op jit(solution)/shard_map/ppermute | solution.py:24
  134.4 1.9 collective-permute-start.13
  137.0 11.8 %all-to-all-start.3 = ((f32[32,1,128]{2,1,0:T(1,128)}), f32[32,1,128]{2,1,0:T(1,128)S(1)}, u32[]{:S(2)}, u32[]{:S(2)}) async-start(f32[32,1,128]{2,1,0:T(1,128)} %bitcast.16), calls=%async_computation.3 | async-start | bytes 32768 | tf_op jit(solution)/shard_map/all_to_all | solution.py:307
  148.8 4.3 %copy-done.1 = bf16[10,768,768]{2,1,0:T(8,128)(2,1)S(1)} copy-done((bf16[10,768,768]{2,1,0:T(8,128)(2,1)S(1)}, bf16[10,768,768]{2,1,0:T(8,128)(2,1)}, u32[]{:S(2)}) %copy-start.1) | copy-done | bytes 11796504
  155.4 5.9 %shard_map.119.base_ref = f32[256,768]{1,0:T(8,128)S(1)} custom-call(s32[256,1]{1,0:T(8,128)S(1)} %copy.57.ident_ref, f32[256,768]{1,0:T(8,128)S(1)} %copy-done.6, f32[256,768]{1,0:T(8,128)S(1)} %copy-done.10, bf16[10,768,768]{2,1,0:T(8,128)(2,1)S(1)} %copy-done.1), custom_call_target="tpu_custom_call" | custom-call | flops 3019898880 | bytes 11796480 | tf_op jit(solution)/shard_map/pallas_call | solution.py:222
  162.5 1.4 copy.62
  167.5 11.1 %shard_map.120 = (f32[256,768]{1,0:T(8,128)S(1)}, f32[256,128]{1,0:T(8,128)S(1)}) custom-call(f32[2048,128]{1,0:T(8,128)} %bitcast.13.got_ref, f32[2048,128]{1,0:T(8,128)S(1)} %copy-done.4, f32[2048,2]{1,0:T(8,128)S(1)} %broadcast_multiply_fusion.shift_ref, s32[2048,4]{1,0:T(8,128)S(1)} %copy.56.cols_ref, f32[2048,2]{1,0:T(8,128)S(1)} %copy.60.conduct_ref, ...), custom_call_target="tpu_custom_call" | custom-call | tf_op jit(solution)/shard_map/pallas_call | solution.py:243
  179.6 3.3 %collective-permute-start.8 = (f32[4,32,32]{2,1,0:T(8,128)S(1)}, f32[4,32,32]{2,1,0:T(8,128)S(1)}, u32[]{:S(2)}, u32[]{:S(2)}) collective-permute-start(f32[4,32,32]{2,1,0:T(8,128)S(1)} %slice.350), channel_id=1, source_target_pairs={{0,4},{4,8},{8,12},{12,16},{16,20},{20,24},{24,28},{1,5},{5,9},{9,... | collective-permute-start | bytes 49160 | tf_op jit(solution)/shard_map/ppermute | solution.py:24
  184.0 3.1 %collective-permute-start.14 = (f32[40,4,32]{2,1,0:T(4,128)S(1)}, f32[40,4,32]{2,1,0:T(4,128)S(1)}, u32[]{:S(2)}, u32[]{:S(2)}) collective-permute-start(f32[40,4,32]{2,1,0:T(4,128)S(1)} %get-tuple-element.34), channel_id=1, source_target_pairs={{0,1},{1,2},{2,3},{4,5},{5,6},{6,7},{8,9},{9,10},{10,11},{12,13},{... | collective-permute-start | bytes 61448 | tf_op jit(solution)/shard_map/ppermute | solution.py:24
  188.6 2.1 %collective-permute-start.9 = (f32[4,32,32]{2,1,0:T(8,128)S(1)}, f32[4,32,32]{2,1,0:T(8,128)S(1)}, u32[]{:S(2)}, u32[]{:S(2)}) collective-permute-start(f32[4,32,32]{2,1,0:T(8,128)S(1)} %slice.352), channel_id=1, source_target_pairs={{4,0},{8,4},{12,8},{16,12},{20,16},{24,20},{28,24},{5,1},{9,5},{13... | collective-permute-start | bytes 49160 | tf_op jit(solution)/shard_map/ppermute | solution.py:25
  190.8 4.3 %collective-permute-done.9 = f32[4,32,32]{2,1,0:T(8,128)S(1)} collective-permute-done((f32[4,32,32]{2,1,0:T(8,128)S(1)}, f32[4,32,32]{2,1,0:T(8,128)S(1)}, u32[]{:S(2)}, u32[]{:S(2)}) %collective-permute-start.9) | collective-permute-done | bytes 16416 | tf_op jit(solution)/shard_map/ppermute | solution.py:25
  195.1 4.0 %collective-permute-start.10 = (f32[40,4,32]{2,1,0:T(4,128)S(1)}, f32[40,4,32]{2,1,0:T(4,128)S(1)}, u32[]{:S(2)}, u32[]{:S(2)}) collective-permute-start(f32[40,4,32]{2,1,0:T(4,128)S(1)} %get-tuple-element.32), channel_id=1, source_target_pairs={{0,1},{1,2},{2,3},{4,5},{5,6},{6,7},{8,9},{9,10},{10,11},{12,13},{... | collective-permute-start | bytes 61448 | tf_op jit(solution)/shard_map/ppermute | solution.py:24
  201.6 2.7 %collective-permute-done.11 = f32[40,4,32]{2,1,0:T(4,128)S(1)} collective-permute-done((f32[40,4,32]{2,1,0:T(4,128)S(1)}, f32[40,4,32]{2,1,0:T(4,128)S(1)}, u32[]{:S(2)}, u32[]{:S(2)}) %collective-permute-start.11) | collective-permute-done | bytes 20512 | tf_op jit(solution)/shard_map/ppermute | solution.py:25
  207.2 4.9 %shard_map.121 = (f32[256,768]{1,0:T(8,128)}, f32[256,768]{1,0:T(8,128)}, f32[128,256]{1,0:T(8,128)}) custom-call(f32[256,768]{1,0:T(8,128)S(1)} %copy-done.6, f32[256,768]{1,0:T(8,128)S(1)} %copy-done.11, f32[256,768]{1,0:T(8,128)S(1)} %copy-done.19, f32[256,128]{1,0:T(8,128)S(1)} %reshape.495.phi_ref, s32[256,12]{1,0:T(8,128)S(1)} %reshape.488.memb_ref), custom_call_target="tpu_custom_call" | custom-call | tf_op jit(solution)/shard_map/pallas_call | solution.py:270
  (185 shorter events, 58.5 us)
Async XLA Ops:
  0.6 14.9 %copy-start.23 = (f32[32,32,32]{2,1,0:T(8,128)S(1)}, f32[32,32,32]{2,1,0:T(8,128)}, u32[]{:S(2)}) copy-start(f32[32,32,32]{2,1,0:T(8,128)} %param.12) | copy-start | bytes 393220
  0.6 25.1 %copy-start.2 = (f32[256,768]{1,0:T(8,128)S(1)}, f32[256,768]{1,0:T(8,128)}, u32[]{:S(2)}) copy-start(f32[256,768]{1,0:T(8,128)} %volt_ref.7) | copy-start | bytes 2359300
  6.4 32.2 %copy-start.33 = (s32[256]{0:T(256)S(1)}, s32[256]{0:T(256)}, u32[]{:S(2)}) copy-start(s32[256]{0:T(256)} %param.14) | copy-start | bytes 3076
  6.5 32.4 %copy-start.7 = (f32[256,768]{1,0:T(8,128)S(1)}, f32[256,768]{1,0:T(8,128)}, u32[]{:S(2)}) copy-start(f32[256,768]{1,0:T(8,128)} %recov_ref.3) | copy-start | bytes 2359300
  9.1 15.7 %all-to-all-start = ((f32[32,1,128]{2,1,0:T(1,128)}), f32[32,1,128]{2,1,0:T(1,128)S(1)}, u32[]{:S(2)}, u32[]{:S(2)}) async-start(f32[32,1,128]{2,1,0:T(1,128)} %bitcast.2), calls=%async_computation | async-start | bytes 32768 | tf_op jit(solution)/shard_map/all_to_all | solution.py:307
  16.2 34.7 %collective-permute-start.4 = (f32[4,32,32]{2,1,0:T(8,128)}, f32[4,32,32]{2,1,0:T(8,128)}, u32[]{:S(2)}, u32[]{:S(2)}) collective-permute-start(f32[4,32,32]{2,1,0:T(8,128)} %get-tuple-element.43), channel_id=1, source_target_pairs={{0,4},{4,8},{8,12},{12,16},{16,20},{20,24},{24,28},{1,5},{5,9},{9,... | collective-permute-start | bytes 49160 | tf_op jit(solution)/shard_map/ppermute | solution.py:24
  19.5 32.2 %collective-permute-start.5 = (f32[4,32,32]{2,1,0:T(8,128)}, f32[4,32,32]{2,1,0:T(8,128)S(1)}, u32[]{:S(2)}, u32[]{:S(2)}) collective-permute-start(f32[4,32,32]{2,1,0:T(8,128)} %get-tuple-element.42), channel_id=1, source_target_pairs={{4,0},{8,4},{12,8},{16,12},{20,16},{24,20},{28,24},{5,1},{9,5},{13... | collective-permute-start | bytes 49160 | tf_op jit(solution)/shard_map/ppermute | solution.py:25
  24.8 24.3 %copy-start.30 = (pred[32,64]{1,0:T(8,128)(4,1)}, pred[32,64]{1,0:T(8,128)(4,1)S(1)}, u32[]{:S(2)}) copy-start(pred[32,64]{1,0:T(8,128)(4,1)S(1)} %get-tuple-element.53) | copy-start | bytes 6148
  24.8 24.3 %copy-start.31 = (pred[32,64]{1,0:T(8,128)(4,1)}, pred[32,64]{1,0:T(8,128)(4,1)S(1)}, u32[]{:S(2)}) copy-start(pred[32,64]{1,0:T(8,128)(4,1)S(1)} %get-tuple-element.54) | copy-start | bytes 6148
  32.4 32.5 %all-to-all-start.1 = ((f32[32,64,128]{2,1,0:T(8,128)}), f32[32,64,128]{2,1,0:T(8,128)}, u32[]{:S(2)}, u32[]{:S(2)}) async-start(f32[32,64,128]{2,1,0:T(8,128)} %bitcast.4), calls=%async_computation.1 | async-start | bytes 2097152 | tf_op jit(solution)/shard_map/all_to_all | solution.py:307
  43.2 7.5 %copy-start.32 = (s32[3072]{0:T(1024)S(1)}, s32[3072]{0:T(1024)}, u32[]{:S(2)}) copy-start(s32[3072]{0:T(1024)} %param.19) | copy-start | bytes 36868
  53.3 50.8 %collective-permute-start.6 = (f32[40,4,32]{2,1,0:T(4,128)}, f32[40,4,32]{2,1,0:T(4,128)S(1)}, u32[]{:S(2)}, u32[]{:S(2)}) collective-permute-start(f32[40,4,32]{2,1,0:T(4,128)} %get-tuple-element.38), channel_id=1, source_target_pairs={{0,1},{1,2},{2,3},{4,5},{5,6},{6,7},{8,9},{9,10},{10,11},{12,13},{... | collective-permute-start | bytes 61448 | tf_op jit(solution)/shard_map/ppermute | solution.py:24
  56.4 47.7 %collective-permute-start.7 = (f32[40,4,32]{2,1,0:T(4,128)}, f32[40,4,32]{2,1,0:T(4,128)S(1)}, u32[]{:S(2)}, u32[]{:S(2)}) collective-permute-start(f32[40,4,32]{2,1,0:T(4,128)} %get-tuple-element.39), channel_id=1, source_target_pairs={{1,0},{2,1},{3,2},{5,4},{6,5},{7,6},{9,8},{10,9},{11,10},{13,12},{... | collective-permute-start | bytes 61448 | tf_op jit(solution)/shard_map/ppermute | solution.py:25
  77.3 6.0 %copy-start.12 = (f32[256,768]{1,0:T(8,128)}, f32[256,768]{1,0:T(8,128)S(1)}, u32[]{:S(2)}) copy-start(f32[256,768]{1,0:T(8,128)S(1)} %get-tuple-element.14.volt_ref.early_ref) | copy-start | bytes 2359300
  85.1 12.7 %collective-permute-start = (f32[4,32,32]{2,1,0:T(8,128)S(1)}, f32[4,32,32]{2,1,0:T(8,128)}, u32[]{:S(2)}, u32[]{:S(2)}) collective-permute-start(f32[4,32,32]{2,1,0:T(8,128)S(1)} %slice.309), channel_id=1, source_target_pairs={{0,4},{4,8},{8,12},{12,16},{16,20},{20,24},{24,28},{1,5},{5,9},{9,... | collective-permute-start | bytes 49160 | tf_op jit(solution)/shard_map/ppermute | solution.py:24
  89.5 10.2 %collective-permute-start.1 = (f32[4,32,32]{2,1,0:T(8,128)S(1)}, f32[4,32,32]{2,1,0:T(8,128)S(1)}, u32[]{:S(2)}, u32[]{:S(2)}) collective-permute-start(f32[4,32,32]{2,1,0:T(8,128)S(1)} %slice.311), channel_id=1, source_target_pairs={{4,0},{8,4},{12,8},{16,12},{20,16},{24,20},{28,24},{5,1},{9,5},{13... | collective-permute-start | bytes 49160 | tf_op jit(solution)/shard_map/ppermute | solution.py:25
  92.1 44.2 %all-to-all-start.2 = ((f32[32,64,128]{2,1,0:T(8,128)}), f32[32,64,128]{2,1,0:T(8,128)}, u32[]{:S(2)}, u32[]{:S(2)}) async-start(f32[32,64,128]{2,1,0:T(8,128)} %bitcast.40), calls=%async_computation.2 | async-start | bytes 2097152 | tf_op jit(solution)/shard_map/all_to_all | solution.py:307
  97.7 18.8 %copy-start.24 = (pred[38,38]{1,0:T(8,128)(4,1)S(1)}, pred[38,38]{1,0:T(8,128)(4,1)}, u32[]{:S(2)}) copy-start(pred[38,38]{1,0:T(8,128)(4,1)} %broadcast_and_fusion) | copy-start | bytes 4336
  99.7 16.7 %collective-permute-start.2 = (f32[40,4,32]{2,1,0:T(4,128)S(1)}, f32[40,4,32]{2,1,0:T(4,128)S(1)}, u32[]{:S(2)}, u32[]{:S(2)}) collective-permute-start(f32[40,4,32]{2,1,0:T(4,128)S(1)} %get-tuple-element.36), channel_id=1, source_target_pairs={{0,1},{1,2},{2,3},{4,5},{5,6},{6,7},{8,9},{9,10},{10,11},{12,13},{... | collective-permute-start | bytes 61448 | tf_op jit(solution)/shard_map/ppermute | solution.py:24
  102.8 14.4 %copy-start.26 = (pred[36,36]{1,0:T(8,128)(4,1)S(1)}, pred[36,36]{1,0:T(8,128)(4,1)}, u32[]{:S(2)}) copy-start(pred[36,36]{1,0:T(8,128)(4,1)} %broadcast_and_fusion.1) | copy-start | bytes 3892
  102.8 13.6 %collective-permute-start.3 = (f32[40,4,32]{2,1,0:T(4,128)S(1)}, f32[40,4,32]{2,1,0:T(4,128)S(1)}, u32[]{:S(2)}, u32[]{:S(2)}) collective-permute-start(f32[40,4,32]{2,1,0:T(4,128)S(1)} %get-tuple-element.37), channel_id=1, source_target_pairs={{1,0},{2,1},{3,2},{5,4},{6,5},{7,6},{9,8},{10,9},{11,10},{13,12},{... | collective-permute-start | bytes 61448 | tf_op jit(solution)/shard_map/ppermute | solution.py:25
  130.5 52.4 %collective-permute-start.12 = (f32[4,32,32]{2,1,0:T(8,128)S(1)}, f32[4,32,32]{2,1,0:T(8,128)S(1)}, u32[]{:S(2)}, u32[]{:S(2)}) collective-permute-start(f32[4,32,32]{2,1,0:T(8,128)S(1)} %get-tuple-element.40), channel_id=1, source_target_pairs={{0,4},{4,8},{8,12},{12,16},{16,20},{20,24},{24,28},{1,5},{5,9},{9,... | collective-permute-start | bytes 49160 | tf_op jit(solution)/shard_map/ppermute | solution.py:24
  134.4 48.6 %collective-permute-start.13 = (f32[4,32,32]{2,1,0:T(8,128)S(1)}, f32[4,32,32]{2,1,0:T(8,128)S(1)}, u32[]{:S(2)}, u32[]{:S(2)}) collective-permute-start(f32[4,32,32]{2,1,0:T(8,128)S(1)} %get-tuple-element.41), channel_id=1, source_target_pairs={{4,0},{8,4},{12,8},{16,12},{20,16},{24,20},{28,24},{5,1},{9,5},{13... | collective-permute-start | bytes 49160 | tf_op jit(solution)/shard_map/ppermute | solution.py:25
  137.0 25.2 %all-to-all-start.3 = ((f32[32,1,128]{2,1,0:T(1,128)}), f32[32,1,128]{2,1,0:T(1,128)S(1)}, u32[]{:S(2)}, u32[]{:S(2)}) async-start(f32[32,1,128]{2,1,0:T(1,128)} %bitcast.16), calls=%async_computation.3 | async-start | bytes 32768 | tf_op jit(solution)/shard_map/all_to_all | solution.py:307
  179.5 25.0 %copy-start.25 = (pred[38,38]{1,0:T(8,128)(4,1)S(1)}, pred[38,38]{1,0:T(8,128)(4,1)}, u32[]{:S(2)}) copy-start(pred[38,38]{1,0:T(8,128)(4,1)} %broadcast_and_fusion) | copy-start | bytes 4336
  179.6 11.2 %collective-permute-start.8 = (f32[4,32,32]{2,1,0:T(8,128)S(1)}, f32[4,32,32]{2,1,0:T(8,128)S(1)}, u32[]{:S(2)}, u32[]{:S(2)}) collective-permute-start(f32[4,32,32]{2,1,0:T(8,128)S(1)} %slice.350), channel_id=1, source_target_pairs={{0,4},{4,8},{8,12},{12,16},{16,20},{20,24},{24,28},{1,5},{5,9},{9,... | collective-permute-start | bytes 49160 | tf_op jit(solution)/shard_map/ppermute | solution.py:24
  184.0 16.5 %collective-permute-start.14 = (f32[40,4,32]{2,1,0:T(4,128)S(1)}, f32[40,4,32]{2,1,0:T(4,128)S(1)}, u32[]{:S(2)}, u32[]{:S(2)}) collective-permute-start(f32[40,4,32]{2,1,0:T(4,128)S(1)} %get-tuple-element.34), channel_id=1, source_target_pairs={{0,1},{1,2},{2,3},{4,5},{5,6},{6,7},{8,9},{9,10},{10,11},{12,13},{... | collective-permute-start | bytes 61448 | tf_op jit(solution)/shard_map/ppermute | solution.py:24
  187.1 13.4 %collective-permute-start.15 = (f32[40,4,32]{2,1,0:T(4,128)S(1)}, f32[40,4,32]{2,1,0:T(4,128)S(1)}, u32[]{:S(2)}, u32[]{:S(2)}) collective-permute-start(f32[40,4,32]{2,1,0:T(4,128)S(1)} %get-tuple-element.35), channel_id=1, source_target_pairs={{1,0},{2,1},{3,2},{5,4},{6,5},{7,6},{9,8},{10,9},{11,10},{13,12},{... | collective-permute-start | bytes 61448 | tf_op jit(solution)/shard_map/ppermute | solution.py:25
  188.6 6.5 %collective-permute-start.9 = (f32[4,32,32]{2,1,0:T(8,128)S(1)}, f32[4,32,32]{2,1,0:T(8,128)S(1)}, u32[]{:S(2)}, u32[]{:S(2)}) collective-permute-start(f32[4,32,32]{2,1,0:T(8,128)S(1)} %slice.352), channel_id=1, source_target_pairs={{4,0},{8,4},{12,8},{16,12},{20,16},{24,20},{28,24},{5,1},{9,5},{13... | collective-permute-start | bytes 49160 | tf_op jit(solution)/shard_map/ppermute | solution.py:25
  195.1 6.5 %collective-permute-start.10 = (f32[40,4,32]{2,1,0:T(4,128)S(1)}, f32[40,4,32]{2,1,0:T(4,128)S(1)}, u32[]{:S(2)}, u32[]{:S(2)}) collective-permute-start(f32[40,4,32]{2,1,0:T(4,128)S(1)} %get-tuple-element.32), channel_id=1, source_target_pairs={{0,1},{1,2},{2,3},{4,5},{5,6},{6,7},{8,9},{9,10},{10,11},{12,13},{... | collective-permute-start | bytes 61448 | tf_op jit(solution)/shard_map/ppermute | solution.py:24
  199.1 6.0 %copy-start.27 = (pred[36,36]{1,0:T(8,128)(4,1)S(1)}, pred[36,36]{1,0:T(8,128)(4,1)}, u32[]{:S(2)}) copy-start(pred[36,36]{1,0:T(8,128)(4,1)} %broadcast_and_fusion.1) | copy-start | bytes 3892
  199.1 5.2 %collective-permute-start.11 = (f32[40,4,32]{2,1,0:T(4,128)S(1)}, f32[40,4,32]{2,1,0:T(4,128)S(1)}, u32[]{:S(2)}, u32[]{:S(2)}) collective-permute-start(f32[40,4,32]{2,1,0:T(4,128)S(1)} %get-tuple-element.33), channel_id=1, source_target_pairs={{1,0},{2,1},{3,2},{5,4},{6,5},{7,6},{9,8},{10,9},{11,10},{13,12},{... | collective-permute-start | bytes 61448 | tf_op jit(solution)/shard_map/ppermute | solution.py:25
  (22 other events, 34.8 us)

commit v3 on v0

--- a/solution.py
+++ b/solution.py
@@ -311,15 +311,14 @@
         sent = gather(volt, cols, slots, rows_at_once)
         got = exchange(sent.reshape(devices, capacity, LANES)).reshape(slots, LANES)
         base = steklov(ident, volt, recov, templates)
+        depth = SWEEPS
+        framed_phi = extended(phi, (("tx", 0), ("ty", 1)), depth)
+        got, framed_phi = lax.optimization_barrier((got, framed_phi))
         current, deposit = scatter(
             got, sent, cols, conduct_cols, cell_rows, base, memb, memb_t, points // LANES, rows_at_once
         )
         deposit = deposit.reshape(ecs_start.shape)
-        depth = SWEEPS
-        framed_phi, framed_dep = (
-            extended(phi, (("tx", 0), ("ty", 1)), depth),
-            extended(deposit, (("tx", 0), ("ty", 1)), depth),
-        )
+        framed_dep = extended(deposit, (("tx", 0), ("ty", 1)), depth)
         current_phi = framed_phi
         for sweep in range(SWEEPS):
             rim = depth - sweep - 1

time: 197 us -> 199 us (1.010)
  waiting for transfers between devices: 29.2 us -> 39.8 us
  local copies, waits for them, and re-layouts: 34.5 us -> 26.5 us
  other arithmetic: 17.4 us -> 14.7 us
    ppermute x8, waiting for transfers between devices: 0.02 us -> 14.1 us  [extended(): before = lax.ppermute(last, axis, up)]
    all_to_all x3, waiting for transfers between devices: 17.1 us -> 5.57 us  [exchange(): lax.all_to_all(x, ('tx', 'ty'), split_axis=0, concat_axis=0, tiled=True)]
    ppermute x8, waiting for transfers between devices: 12 us -> 20.2 us  [extended(): after = lax.ppermute(leading, axis, down)]
    slice x6, local copies, waits for them, and re-layouts: 3.38 us -> 0.26 us  [extended(): last = lax.slice_in_dim(x, length - width, length, axis=dim)]
    and x4, other arithmetic: 2.67 us -> 0.3 us  [on_device(): inside = inside_x[:, None, None] & inside_y[None, :, None]]
    unnamed x60 -> x58, local copies, waits for them, and re-layouts: 22.2 us -> 20 us
  transfers between devices with their start and end apart: 19 -> 19, of which waited for: 6 -> 8; matrix products, arithmetic and copies ran while one was open for 9% -> 4% of each run, Pallas kernels for 15% -> 9%
where the time goes in v3:
time: 199 us; the launch traced here: 197 us
  starting transfers between devices  56.9 us (29%)
  Pallas kernels  54.4 us (27%)
  waiting for transfers between devices  39.8 us (20%)
  local copies, waits for them, and re-layouts  26.5 us (13%)
  other arithmetic  14.7 us (7%)
  matrix products  2.85 us (1%)
    ppermute x8, starting transfers between devices, extended(): before = lax.ppermute(last, axis, up)  27.9 us
    pallas_call x2, Pallas kernels, scatter(): pl.pallas_call(scatter_kernel, grid=(slots // tile,), in_specs=[pl.BlockS...  21.2 us
    ppermute x8, waiting for transfers between devices, extended(): after = lax.ppermute(leading, axis, down)  20.2 us
    unnamed x58, local copies, waits for them, and re-layouts  20 us
    ppermute x8, starting transfers between devices, extended(): after = lax.ppermute(leading, axis, down)  14.7 us
    all_to_all x3, starting transfers between devices, exchange(): lax.all_to_all(x, ('tx', 'ty'), split_axis=0, concat_axis=0, tiled=True)  14.3 us
    ppermute x8, waiting for transfers between devices, extended(): before = lax.ppermute(last, axis, up)  14.1 us
    pallas_call x2, Pallas kernels, gather(): pl.pallas_call(gather_kernel, grid=(slots // tile,), in_specs=[whole_bloc...  13.5 us
  transfers between devices with their start and end apart: 19, of which 8 were waited for; matrix products, arithmetic and copies ran while one was open for 4% of the time, Pallas kernels for 9%

profile of v3, /device:TPU:3, one launch (start us, length us, event | category | flops | bytes accessed | tf_op | source)
XLA Modules:
  0.0 196.7 jit_solution(620475191708237341)
XLA Ops:
  8.5 6.4 %all-to-all-start = ((f32[32,1,128]{2,1,0:T(1,128)}), f32[32,1,128]{2,1,0:T(1,128)S(1)}, u32[]{:S(2)}, u32[]{:S(2)}) async-start(f32[32,1,128]{2,1,0:T(1,128)} %bitcast.2), calls=%async_computation | async-start | bytes 32768 | tf_op jit(solution)/shard_map/all_to_all | solution.py:264
  15.0 2.3 %collective-permute-start.1 = (f32[4,32,32]{2,1,0:T(8,128)S(1)}, f32[4,32,32]{2,1,0:T(8,128)S(1)}, u32[]{:S(2)}, u32[]{:S(2)}) collective-permute-start(f32[4,32,32]{2,1,0:T(8,128)S(1)} %get-tuple-element.40), channel_id=1, source_target_pairs={{4,0},{8,4},{12,8},{16,12},{20,16},{24,20},{28,24},{5,1},{9,5},{13... | collective-permute-start | bytes 49160 | tf_op jit(solution)/shard_map/ppermute | solution.py:23
  17.3 4.2 %collective-permute-start = (f32[4,32,32]{2,1,0:T(8,128)S(1)}, f32[4,32,32]{2,1,0:T(8,128)S(1)}, u32[]{:S(2)}, u32[]{:S(2)}) collective-permute-start(f32[4,32,32]{2,1,0:T(8,128)S(1)} %get-tuple-element.41), channel_id=1, source_target_pairs={{0,4},{4,8},{8,12},{12,16},{16,20},{20,24},{24,28},{1,5},{5,9},{9,... | collective-permute-start | bytes 49160 | tf_op jit(solution)/shard_map/ppermute | solution.py:22
  21.9 4.3 %copy-done = bf16[10,768,768]{2,1,0:T(8,128)(2,1)S(1)} copy-done((bf16[10,768,768]{2,1,0:T(8,128)(2,1)S(1)}, bf16[10,768,768]{2,1,0:T(8,128)(2,1)}, u32[]{:S(2)}) %copy-start) | copy-done | bytes 11796504
  26.2 5.9 %shard_map.114.base_ref = f32[256,768]{1,0:T(8,128)S(1)} custom-call(s32[256,1]{1,0:T(8,128)S(1)} %copy.44.ident_ref, f32[256,768]{1,0:T(8,128)S(1)} %copy-done.2, f32[256,768]{1,0:T(8,128)S(1)} %copy-done.8, bf16[10,768,768]{2,1,0:T(8,128)(2,1)S(1)} %copy-done), custom_call_target="tpu_custom_call" | custom-call | flops 3019898880 | bytes 11796480 | tf_op jit(solution)/shard_map/pallas_call | solution.py:190
  33.9 6.7 %shard_map.113.sent_ref = f32[2048,128]{1,0:T(8,128)} custom-call(f32[256,768]{1,0:T(8,128)S(1)} %copy-done.2, s32[2048,4]{1,0:T(8,128)S(1)} %copy.43.cols_ref), custom_call_target="tpu_custom_call" | custom-call | tf_op jit(solution)/shard_map/pallas_call | solution.py:176
  40.6 4.7 %all-to-all-start.1 = ((f32[32,64,128]{2,1,0:T(8,128)}), f32[32,64,128]{2,1,0:T(8,128)}, u32[]{:S(2)}, u32[]{:S(2)}) async-start(f32[32,64,128]{2,1,0:T(8,128)} %bitcast.4), calls=%async_computation.1 | async-start | bytes 2097152 | tf_op jit(solution)/shard_map/all_to_all | solution.py:264
  46.7 3.1 %collective-permute-start.2 = (f32[40,4,32]{2,1,0:T(4,128)S(1)}, f32[40,4,32]{2,1,0:T(4,128)S(1)}, u32[]{:S(2)}, u32[]{:S(2)}) collective-permute-start(f32[40,4,32]{2,1,0:T(4,128)S(1)} %get-tuple-element.36), channel_id=1, source_target_pairs={{0,1},{1,2},{2,3},{4,5},{5,6},{6,7},{8,9},{9,10},{10,11},{12,13},{... | collective-permute-start | bytes 61448 | tf_op jit(solution)/shard_map/ppermute | solution.py:22
  52.0 12.1 %collective-permute-done.2 = f32[40,4,32]{2,1,0:T(4,128)S(1)} collective-permute-done((f32[40,4,32]{2,1,0:T(4,128)S(1)}, f32[40,4,32]{2,1,0:T(4,128)S(1)}, u32[]{:S(2)}, u32[]{:S(2)}) %collective-permute-start.2) | collective-permute-done | bytes 20512 | tf_op jit(solution)/shard_map/ppermute | solution.py:22
  64.1 2.1 %pad_maximum_fusion = f32[40,40,32]{2,1,0:T(8,128)} fusion(f32[40,4,32]{2,1,0:T(4,128)S(1)} %collective-permute-done.3, f32[40,32,32]{2,1,0:T(8,128)} %copy-done.22, f32[40,4,32]{2,1,0:T(4,128)S(1)} %collective-permute-done.2), kind=kLoop, calls=%fused_computation.8 | loop fusion | flops 102400 | bytes 409600 | tf_op jit(solution)/shard_map/concatenate | solution.py:24
  66.1 5.6 %all-to-all-done.1 = f32[32,64,128]{2,1,0:T(8,128)} async-done(((f32[32,64,128]{2,1,0:T(8,128)}), f32[32,64,128]{2,1,0:T(8,128)}, u32[]{:S(2)}, u32[]{:S(2)}) %all-to-all-start.1) | async-done | bytes 1048608 | tf_op jit(solution)/shard_map/all_to_all | solution.py:264
  72.8 10.6 %shard_map.115 = (f32[256,768]{1,0:T(8,128)S(1)}, f32[256,128]{1,0:T(8,128)S(1)}) custom-call(f32[2048,128]{1,0:T(8,128)} %bitcast.5.got_ref, f32[2048,128]{1,0:T(8,128)} %shard_map.113.sent_ref, s32[2048,4]{1,0:T(8,128)S(1)} %copy.43.cols_ref, f32[2048,2]{1,0:T(8,128)S(1)} %copy.47.conduct_ref, s32[2,2048]{1,0:T(2,128)S(1)} %pad_add_fusion.1.cells_ref, ...), custom_call_target="tpu_custom_call" | custom-call | tf_op jit(solution)/shard_map/pallas_call | solution.py:211
  87.4 2.5 %collective-permute-start.5 = (f32[4,32,32]{2,1,0:T(8,128)S(1)}, f32[4,32,32]{2,1,0:T(8,128)S(1)}, u32[]{:S(2)}, u32[]{:S(2)}) collective-permute-start(f32[4,32,32]{2,1,0:T(8,128)S(1)} %slice.301), channel_id=1, source_target_pairs={{4,0},{8,4},{12,8},{16,12},{20,16},{24,20},{28,24},{5,1},{9,5},{13... | collective-permute-start | bytes 49160 | tf_op jit(solution)/shard_map/ppermute | solution.py:23
  91.0 3.0 %collective-permute-done.5 = f32[4,32,32]{2,1,0:T(8,128)S(1)} collective-permute-done((f32[4,32,32]{2,1,0:T(8,128)S(1)}, f32[4,32,32]{2,1,0:T(8,128)S(1)}, u32[]{:S(2)}, u32[]{:S(2)}) %collective-permute-start.5) | collective-permute-done | bytes 16416 | tf_op jit(solution)/shard_map/ppermute | solution.py:23
  94.0 7.0 %collective-permute-start.6 = (f32[40,4,32]{2,1,0:T(4,128)S(1)}, f32[40,4,32]{2,1,0:T(4,128)S(1)}, u32[]{:S(2)}, u32[]{:S(2)}) collective-permute-start(f32[40,4,32]{2,1,0:T(4,128)S(1)} %get-tuple-element.34), channel_id=1, source_target_pairs={{0,1},{1,2},{2,3},{4,5},{5,6},{6,7},{8,9},{9,10},{10,11},{12,13},{... | collective-permute-start | bytes 61448 | tf_op jit(solution)/shard_map/ppermute | solution.py:22
  102.6 3.6 %collective-permute-done.7 = f32[40,4,32]{2,1,0:T(4,128)S(1)} collective-permute-done((f32[40,4,32]{2,1,0:T(4,128)S(1)}, f32[40,4,32]{2,1,0:T(4,128)S(1)}, u32[]{:S(2)}, u32[]{:S(2)}) %collective-permute-start.7) | collective-permute-done | bytes 20512 | tf_op jit(solution)/shard_map/ppermute | solution.py:23
  113.1 3.5 %shard_map.116 = (f32[256,768]{1,0:T(8,128)S(1)}, f32[256,768]{1,0:T(8,128)S(1)}) custom-call(f32[256,768]{1,0:T(8,128)S(1)} %copy-done.2, f32[256,768]{1,0:T(8,128)S(1)} %copy-done.9, f32[256,768]{1,0:T(8,128)S(1)} %copy-done.16, f32[256,128]{1,0:T(8,128)S(1)} %reshape.448.phi_ref, s32[256,12]{1,0:T(8,128)S(1)} %reshape.446.memb_ref), custom_call_target="tpu_custom_call" | custom-call | tf_op jit(solution)/shard_map/pallas_call | solution.py:235
  116.6 6.7 %shard_map.117.sent_ref = f32[2048,128]{1,0:T(8,128)} custom-call(f32[256,768]{1,0:T(8,128)S(1)} %get-tuple-element.17.volt_ref, s32[2048,4]{1,0:T(8,128)S(1)} %copy.43.cols_ref), custom_call_target="tpu_custom_call" | custom-call | tf_op jit(solution)/shard_map/pallas_call | solution.py:176
  124.3 3.1 %all-to-all-start.2 = ((f32[32,64,128]{2,1,0:T(8,128)}), f32[32,64,128]{2,1,0:T(8,128)}, u32[]{:S(2)}, u32[]{:S(2)}) async-start(f32[32,64,128]{2,1,0:T(8,128)} %bitcast.11), calls=%async_computation.2 | async-start | bytes 2097152 | tf_op jit(solution)/shard_map/all_to_all | solution.py:264
  127.4 3.7 %collective-permute-start.8 = (f32[4,32,32]{2,1,0:T(8,128)S(1)}, f32[4,32,32]{2,1,0:T(8,128)S(1)}, u32[]{:S(2)}, u32[]{:S(2)}) collective-permute-start(f32[4,32,32]{2,1,0:T(8,128)S(1)} %get-tuple-element.38), channel_id=1, source_target_pairs={{0,4},{4,8},{8,12},{12,16},{16,20},{20,24},{24,28},{1,5},{5,9},{9,... | collective-permute-start | bytes 49160 | tf_op jit(solution)/shard_map/ppermute | solution.py:22
  133.0 2.0 %collective-permute-done.8 = f32[4,32,32]{2,1,0:T(8,128)S(1)} collective-permute-done((f32[4,32,32]{2,1,0:T(8,128)S(1)}, f32[4,32,32]{2,1,0:T(8,128)S(1)}, u32[]{:S(2)}, u32[]{:S(2)}) %collective-permute-start.8) | collective-permute-done | bytes 16416 | tf_op jit(solution)/shard_map/ppermute | solution.py:22
  135.0 4.4 %collective-permute-done.9 = f32[4,32,32]{2,1,0:T(8,128)S(1)} collective-permute-done((f32[4,32,32]{2,1,0:T(8,128)S(1)}, f32[4,32,32]{2,1,0:T(8,128)S(1)}, u32[]{:S(2)}, u32[]{:S(2)}) %collective-permute-start.9) | collective-permute-done | bytes 16416 | tf_op jit(solution)/shard_map/ppermute | solution.py:23
  139.4 2.0 %collective-permute-start.10 = (f32[40,4,32]{2,1,0:T(4,128)S(1)}, f32[40,4,32]{2,1,0:T(4,128)S(1)}, u32[]{:S(2)}, u32[]{:S(2)}) collective-permute-start(f32[40,4,32]{2,1,0:T(4,128)S(1)} %get-tuple-element.32), channel_id=1, source_target_pairs={{0,1},{1,2},{2,3},{4,5},{5,6},{6,7},{8,9},{9,10},{10,11},{12,13},{... | collective-permute-start | bytes 61448 | tf_op jit(solution)/shard_map/ppermute | solution.py:22
  142.7 4.3 %copy-done.1 = bf16[10,768,768]{2,1,0:T(8,128)(2,1)S(1)} copy-done((bf16[10,768,768]{2,1,0:T(8,128)(2,1)S(1)}, bf16[10,768,768]{2,1,0:T(8,128)(2,1)}, u32[]{:S(2)}) %copy-start.1) | copy-done | bytes 11796504
  149.3 5.9 %shard_map.118.base_ref = f32[256,768]{1,0:T(8,128)S(1)} custom-call(s32[256,1]{1,0:T(8,128)S(1)} %copy.44.ident_ref, f32[256,768]{1,0:T(8,128)S(1)} %copy-done.4, f32[256,768]{1,0:T(8,128)S(1)} %copy-done.11, bf16[10,768,768]{2,1,0:T(8,128)(2,1)S(1)} %copy-done.1), custom_call_target="tpu_custom_call" | custom-call | flops 3019898880 | bytes 11796480 | tf_op jit(solution)/shard_map/pallas_call | solution.py:190
  156.3 10.6 %shard_map.119 = (f32[256,768]{1,0:T(8,128)S(1)}, f32[256,128]{1,0:T(8,128)S(1)}) custom-call(f32[2048,128]{1,0:T(8,128)} %bitcast.12.got_ref, f32[2048,128]{1,0:T(8,128)} %shard_map.117.sent_ref, s32[2048,4]{1,0:T(8,128)S(1)} %copy.43.cols_ref, f32[2048,2]{1,0:T(8,128)S(1)} %copy.47.conduct_ref, s32[2,2048]{1,0:T(2,128)S(1)} %pad_add_fusion.1.cells_ref, ...), custom_call_target="tpu_custom_call" | custom-call | tf_op jit(solution)/shard_map/pallas_call | solution.py:211
  167.9 2.0 %collective-permute-start.12 = (f32[4,32,32]{2,1,0:T(8,128)S(1)}, f32[4,32,32]{2,1,0:T(8,128)S(1)}, u32[]{:S(2)}, u32[]{:S(2)}) collective-permute-start(f32[4,32,32]{2,1,0:T(8,128)S(1)} %slice.336), channel_id=1, source_target_pairs={{0,4},{4,8},{8,12},{12,16},{16,20},{20,24},{24,28},{1,5},{5,9},{9,... | collective-permute-start | bytes 49160 | tf_op jit(solution)/shard_map/ppermute | solution.py:22
  170.2 2.4 %collective-permute-start.13 = (f32[4,32,32]{2,1,0:T(8,128)S(1)}, f32[4,32,32]{2,1,0:T(8,128)S(1)}, u32[]{:S(2)}, u32[]{:S(2)}) collective-permute-start(f32[4,32,32]{2,1,0:T(8,128)S(1)} %slice.338), channel_id=1, source_target_pairs={{4,0},{8,4},{12,8},{16,12},{20,16},{24,20},{28,24},{5,1},{9,5},{13... | collective-permute-start | bytes 49160 | tf_op jit(solution)/shard_map/ppermute | solution.py:23
  172.7 4.0 %collective-permute-done.13 = f32[4,32,32]{2,1,0:T(8,128)S(1)} collective-permute-done((f32[4,32,32]{2,1,0:T(8,128)S(1)}, f32[4,32,32]{2,1,0:T(8,128)S(1)}, u32[]{:S(2)}, u32[]{:S(2)}) %collective-permute-start.13) | collective-permute-done | bytes 16416 | tf_op jit(solution)/shard_map/ppermute | solution.py:23
  176.7 4.0 %collective-permute-start.14 = (f32[40,4,32]{2,1,0:T(4,128)S(1)}, f32[40,4,32]{2,1,0:T(4,128)S(1)}, u32[]{:S(2)}, u32[]{:S(2)}) collective-permute-start(f32[40,4,32]{2,1,0:T(4,128)S(1)} %get-tuple-element.30), channel_id=1, source_target_pairs={{0,1},{1,2},{2,3},{4,5},{5,6},{6,7},{8,9},{9,10},{10,11},{12,13},{... | collective-permute-start | bytes 61448 | tf_op jit(solution)/shard_map/ppermute | solution.py:22
  182.2 5.2 %collective-permute-done.15 = f32[40,4,32]{2,1,0:T(4,128)S(1)} collective-permute-done((f32[40,4,32]{2,1,0:T(4,128)S(1)}, f32[40,4,32]{2,1,0:T(4,128)S(1)}, u32[]{:S(2)}, u32[]{:S(2)}) %collective-permute-start.15) | collective-permute-done | bytes 20512 | tf_op jit(solution)/shard_map/ppermute | solution.py:23
  192.2 4.5 %shard_map.120 = (f32[256,768]{1,0:T(8,128)}, f32[256,768]{1,0:T(8,128)}) custom-call(f32[256,768]{1,0:T(8,128)S(1)} %copy-done.5, f32[256,768]{1,0:T(8,128)S(1)} %copy-done.12, f32[256,768]{1,0:T(8,128)S(1)} %copy-done.14, f32[256,128]{1,0:T(8,128)S(1)} %reshape.452.phi_ref, s32[256,12]{1,0:T(8,128)S(1)} %reshape.446.memb_ref), custom_call_target="tpu_custom_call" | custom-call | tf_op jit(solution)/shard_map/pallas_call | solution.py:235
  (153 shorter events, 42.8 us)
Async XLA Ops:
  0.6 14.4 %copy-start.23 = (f32[32,32,32]{2,1,0:T(8,128)S(1)}, f32[32,32,32]{2,1,0:T(8,128)}, u32[]{:S(2)}) copy-start(f32[32,32,32]{2,1,0:T(8,128)} %param.12) | copy-start | bytes 393220
  0.6 21.0 %copy-start.25 = (s32[256]{0:T(256)S(1)}, s32[256]{0:T(256)}, u32[]{:S(2)}) copy-start(s32[256]{0:T(256)} %param.14) | copy-start | bytes 3076
  0.6 21.2 %copy-start.2 = (f32[256,768]{1,0:T(8,128)S(1)}, f32[256,768]{1,0:T(8,128)}, u32[]{:S(2)}) copy-start(f32[256,768]{1,0:T(8,128)} %volt_ref.5) | copy-start | bytes 2359300
  0.7 21.2 %copy-start.8 = (f32[256,768]{1,0:T(8,128)S(1)}, f32[256,768]{1,0:T(8,128)}, u32[]{:S(2)}) copy-start(f32[256,768]{1,0:T(8,128)} %recov_ref.3) | copy-start | bytes 2359300
  8.5 24.5 %all-to-all-start = ((f32[32,1,128]{2,1,0:T(1,128)}), f32[32,1,128]{2,1,0:T(1,128)S(1)}, u32[]{:S(2)}, u32[]{:S(2)}) async-start(f32[32,1,128]{2,1,0:T(1,128)} %bitcast.2), calls=%async_computation | async-start | bytes 32768 | tf_op jit(solution)/shard_map/all_to_all | solution.py:264
  15.0 30.8 %collective-permute-start.1 = (f32[4,32,32]{2,1,0:T(8,128)S(1)}, f32[4,32,32]{2,1,0:T(8,128)S(1)}, u32[]{:S(2)}, u32[]{:S(2)}) collective-permute-start(f32[4,32,32]{2,1,0:T(8,128)S(1)} %get-tuple-element.40), channel_id=1, source_target_pairs={{4,0},{8,4},{12,8},{16,12},{20,16},{24,20},{28,24},{5,1},{9,5},{13... | collective-permute-start | bytes 49160 | tf_op jit(solution)/shard_map/ppermute | solution.py:23
  17.3 28.5 %collective-permute-start = (f32[4,32,32]{2,1,0:T(8,128)S(1)}, f32[4,32,32]{2,1,0:T(8,128)S(1)}, u32[]{:S(2)}, u32[]{:S(2)}) collective-permute-start(f32[4,32,32]{2,1,0:T(8,128)S(1)} %get-tuple-element.41), channel_id=1, source_target_pairs={{0,4},{4,8},{8,12},{12,16},{16,20},{20,24},{24,28},{1,5},{5,9},{9,... | collective-permute-start | bytes 49160 | tf_op jit(solution)/shard_map/ppermute | solution.py:22
  21.8 4.4 %copy-start = (bf16[10,768,768]{2,1,0:T(8,128)(2,1)S(1)}, bf16[10,768,768]{2,1,0:T(8,128)(2,1)}, u32[]{:S(2)}) copy-start(bf16[10,768,768]{2,1,0:T(8,128)(2,1)} %template_ref.3) | copy-start | bytes 35389444
  33.0 12.5 %copy-start.24 = (s32[3072]{0:T(1024)S(1)}, s32[3072]{0:T(1024)}, u32[]{:S(2)}) copy-start(s32[3072]{0:T(1024)} %param.19) | copy-start | bytes 36868
  40.6 31.1 %all-to-all-start.1 = ((f32[32,64,128]{2,1,0:T(8,128)}), f32[32,64,128]{2,1,0:T(8,128)}, u32[]{:S(2)}, u32[]{:S(2)}) async-start(f32[32,64,128]{2,1,0:T(8,128)} %bitcast.4), calls=%async_computation.1 | async-start | bytes 2097152 | tf_op jit(solution)/shard_map/all_to_all | solution.py:264
  46.7 17.3 %collective-permute-start.2 = (f32[40,4,32]{2,1,0:T(4,128)S(1)}, f32[40,4,32]{2,1,0:T(4,128)S(1)}, u32[]{:S(2)}, u32[]{:S(2)}) collective-permute-start(f32[40,4,32]{2,1,0:T(4,128)S(1)} %get-tuple-element.36), channel_id=1, source_target_pairs={{0,1},{1,2},{2,3},{4,5},{5,6},{6,7},{8,9},{9,10},{10,11},{12,13},{... | collective-permute-start | bytes 61448 | tf_op jit(solution)/shard_map/ppermute | solution.py:22
  49.8 14.2 %collective-permute-start.3 = (f32[40,4,32]{2,1,0:T(4,128)S(1)}, f32[40,4,32]{2,1,0:T(4,128)S(1)}, u32[]{:S(2)}, u32[]{:S(2)}) collective-permute-start(f32[40,4,32]{2,1,0:T(4,128)S(1)} %get-tuple-element.37), channel_id=1, source_target_pairs={{1,0},{2,1},{3,2},{5,4},{6,5},{7,6},{9,8},{10,9},{11,10},{13,12},{... | collective-permute-start | bytes 61448 | tf_op jit(solution)/shard_map/ppermute | solution.py:23
  84.4 5.5 %collective-permute-start.4 = (f32[4,32,32]{2,1,0:T(8,128)S(1)}, f32[4,32,32]{2,1,0:T(8,128)S(1)}, u32[]{:S(2)}, u32[]{:S(2)}) collective-permute-start(f32[4,32,32]{2,1,0:T(8,128)S(1)} %slice.299), channel_id=1, source_target_pairs={{0,4},{4,8},{8,12},{12,16},{16,20},{20,24},{24,28},{1,5},{5,9},{9,... | collective-permute-start | bytes 49160 | tf_op jit(solution)/shard_map/ppermute | solution.py:22
  87.4 19.0 %copy-start.17 = (f32[40,40,32]{2,1,0:T(8,128)S(1)}, f32[40,40,32]{2,1,0:T(8,128)}, u32[]{:S(2)}) copy-start(f32[40,40,32]{2,1,0:T(8,128)} %pad_maximum_fusion) | copy-start | bytes 614404
  87.4 6.6 %collective-permute-start.5 = (f32[4,32,32]{2,1,0:T(8,128)S(1)}, f32[4,32,32]{2,1,0:T(8,128)S(1)}, u32[]{:S(2)}, u32[]{:S(2)}) collective-permute-start(f32[4,32,32]{2,1,0:T(8,128)S(1)} %slice.301), channel_id=1, source_target_pairs={{4,0},{8,4},{12,8},{16,12},{20,16},{24,20},{28,24},{5,1},{9,5},{13... | collective-permute-start | bytes 49160 | tf_op jit(solution)/shard_map/ppermute | solution.py:23
  94.0 8.6 %collective-permute-start.6 = (f32[40,4,32]{2,1,0:T(4,128)S(1)}, f32[40,4,32]{2,1,0:T(4,128)S(1)}, u32[]{:S(2)}, u32[]{:S(2)}) collective-permute-start(f32[40,4,32]{2,1,0:T(4,128)S(1)} %get-tuple-element.34), channel_id=1, source_target_pairs={{0,1},{1,2},{2,3},{4,5},{5,6},{6,7},{8,9},{9,10},{10,11},{12,13},{... | collective-permute-start | bytes 61448 | tf_op jit(solution)/shard_map/ppermute | solution.py:22
  101.1 5.2 %collective-permute-start.7 = (f32[40,4,32]{2,1,0:T(4,128)S(1)}, f32[40,4,32]{2,1,0:T(4,128)S(1)}, u32[]{:S(2)}, u32[]{:S(2)}) collective-permute-start(f32[40,4,32]{2,1,0:T(4,128)S(1)} %get-tuple-element.35), channel_id=1, source_target_pairs={{1,0},{2,1},{3,2},{5,4},{6,5},{7,6},{9,8},{10,9},{11,10},{13,12},{... | collective-permute-start | bytes 61448 | tf_op jit(solution)/shard_map/ppermute | solution.py:23
  116.6 6.8 %copy-start.10 = (f32[256,768]{1,0:T(8,128)}, f32[256,768]{1,0:T(8,128)S(1)}, u32[]{:S(2)}) copy-start(f32[256,768]{1,0:T(8,128)S(1)} %get-tuple-element.18.recov_ref) | copy-start | bytes 2359300
  116.6 10.8 %copy-start.19 = (f32[32,32,32]{2,1,0:T(8,128)S(1)}, f32[32,32,32]{2,1,0:T(8,128)}, u32[]{:S(2)}) copy-start(f32[32,32,32]{2,1,0:T(8,128)} %fusion.34) | copy-start | bytes 393220
  124.3 32.0 %all-to-all-start.2 = ((f32[32,64,128]{2,1,0:T(8,128)}), f32[32,64,128]{2,1,0:T(8,128)}, u32[]{:S(2)}, u32[]{:S(2)}) async-start(f32[32,64,128]{2,1,0:T(8,128)} %bitcast.11), calls=%async_computation.2 | async-start | bytes 2097152 | tf_op jit(solution)/shard_map/all_to_all | solution.py:264
  127.4 7.6 %collective-permute-start.8 = (f32[4,32,32]{2,1,0:T(8,128)S(1)}, f32[4,32,32]{2,1,0:T(8,128)S(1)}, u32[]{:S(2)}, u32[]{:S(2)}) collective-permute-start(f32[4,32,32]{2,1,0:T(8,128)S(1)} %get-tuple-element.38), channel_id=1, source_target_pairs={{0,4},{4,8},{8,12},{12,16},{16,20},{20,24},{24,28},{1,5},{5,9},{9,... | collective-permute-start | bytes 49160 | tf_op jit(solution)/shard_map/ppermute | solution.py:22
  131.1 8.3 %collective-permute-start.9 = (f32[4,32,32]{2,1,0:T(8,128)S(1)}, f32[4,32,32]{2,1,0:T(8,128)S(1)}, u32[]{:S(2)}, u32[]{:S(2)}) collective-permute-start(f32[4,32,32]{2,1,0:T(8,128)S(1)} %get-tuple-element.39), channel_id=1, source_target_pairs={{4,0},{8,4},{12,8},{16,12},{20,16},{24,20},{28,24},{5,1},{9,5},{13... | collective-permute-start | bytes 49160 | tf_op jit(solution)/shard_map/ppermute | solution.py:23
  139.4 15.8 %collective-permute-start.10 = (f32[40,4,32]{2,1,0:T(4,128)S(1)}, f32[40,4,32]{2,1,0:T(4,128)S(1)}, u32[]{:S(2)}, u32[]{:S(2)}) collective-permute-start(f32[40,4,32]{2,1,0:T(4,128)S(1)} %get-tuple-element.32), channel_id=1, source_target_pairs={{0,1},{1,2},{2,3},{4,5},{5,6},{6,7},{8,9},{9,10},{10,11},{12,13},{... | collective-permute-start | bytes 61448 | tf_op jit(solution)/shard_map/ppermute | solution.py:22
  141.4 13.8 %collective-permute-start.11 = (f32[40,4,32]{2,1,0:T(4,128)S(1)}, f32[40,4,32]{2,1,0:T(4,128)S(1)}, u32[]{:S(2)}, u32[]{:S(2)}) collective-permute-start(f32[40,4,32]{2,1,0:T(4,128)S(1)} %get-tuple-element.33), channel_id=1, source_target_pairs={{1,0},{2,1},{3,2},{5,4},{6,5},{7,6},{9,8},{10,9},{11,10},{13,12},{... | collective-permute-start | bytes 61448 | tf_op jit(solution)/shard_map/ppermute | solution.py:23
  142.7 4.4 %copy-start.1 = (bf16[10,768,768]{2,1,0:T(8,128)(2,1)S(1)}, bf16[10,768,768]{2,1,0:T(8,128)(2,1)}, u32[]{:S(2)}) copy-start(bf16[10,768,768]{2,1,0:T(8,128)(2,1)} %template_ref.3) | copy-start | bytes 35389444
  149.3 5.9 %copy-start.20 = (f32[32,32,32]{2,1,0:T(8,128)S(1)}, f32[32,32,32]{2,1,0:T(8,128)}, u32[]{:S(2)}) copy-start(f32[32,32,32]{2,1,0:T(8,128)} %fusion.34) | copy-start | bytes 393220
  167.8 19.8 %copy-start.18 = (f32[40,40,32]{2,1,0:T(8,128)S(1)}, f32[40,40,32]{2,1,0:T(8,128)}, u32[]{:S(2)}) copy-start(f32[40,40,32]{2,1,0:T(8,128)} %pad_maximum_fusion.2) | copy-start | bytes 614404
  167.9 4.7 %collective-permute-start.12 = (f32[4,32,32]{2,1,0:T(8,128)S(1)}, f32[4,32,32]{2,1,0:T(8,128)S(1)}, u32[]{:S(2)}, u32[]{:S(2)}) collective-permute-start(f32[4,32,32]{2,1,0:T(8,128)S(1)} %slice.336), channel_id=1, source_target_pairs={{0,4},{4,8},{8,12},{12,16},{16,20},{20,24},{24,28},{1,5},{5,9},{9,... | collective-permute-start | bytes 49160 | tf_op jit(solution)/shard_map/ppermute | solution.py:22
  170.2 6.5 %collective-permute-start.13 = (f32[4,32,32]{2,1,0:T(8,128)S(1)}, f32[4,32,32]{2,1,0:T(8,128)S(1)}, u32[]{:S(2)}, u32[]{:S(2)}) collective-permute-start(f32[4,32,32]{2,1,0:T(8,128)S(1)} %slice.338), channel_id=1, source_target_pairs={{4,0},{8,4},{12,8},{16,12},{20,16},{24,20},{28,24},{5,1},{9,5},{13... | collective-permute-start | bytes 49160 | tf_op jit(solution)/shard_map/ppermute | solution.py:23
  176.7 5.5 %collective-permute-start.14 = (f32[40,4,32]{2,1,0:T(4,128)S(1)}, f32[40,4,32]{2,1,0:T(4,128)S(1)}, u32[]{:S(2)}, u32[]{:S(2)}) collective-permute-start(f32[40,4,32]{2,1,0:T(4,128)S(1)} %get-tuple-element.30), channel_id=1, source_target_pairs={{0,1},{1,2},{2,3},{4,5},{5,6},{6,7},{8,9},{9,10},{10,11},{12,13},{... | collective-permute-start | bytes 61448 | tf_op jit(solution)/shard_map/ppermute | solution.py:22
  180.7 6.8 %collective-permute-start.15 = (f32[40,4,32]{2,1,0:T(4,128)S(1)}, f32[40,4,32]{2,1,0:T(4,128)S(1)}, u32[]{:S(2)}, u32[]{:S(2)}) collective-permute-start(f32[40,4,32]{2,1,0:T(4,128)S(1)} %get-tuple-element.31), channel_id=1, source_target_pairs={{1,0},{2,1},{3,2},{5,4},{6,5},{7,6},{9,8},{10,9},{11,10},{13,12},{... | collective-permute-start | bytes 61448 | tf_op jit(solution)/shard_map/ppermute | solution.py:23
  189.0 3.2 %copy-start.5 = (f32[256,768]{1,0:T(8,128)S(1)}, f32[256,768]{1,0:T(8,128)}, u32[]{:S(2)}) copy-start(f32[256,768]{1,0:T(8,128)} %copy-done.3) | copy-start | bytes 2359300
  (13 other events, 17.7 us)
